TPU v7x, 32 devices: a whole 2x2x4 slice. The times are simulated.
32 devices in a mesh: shard: 4 (over y, core), ctx: 4 (over z), tp: 2 (over x).
Axes of the slice: x: 2, y: 2, z: 4, core: 2. Of those that a mesh axis runs over, the one named last changes fastest.
Arguments:
- tokens: bfloat16 [4, 2048, 1024], P('shard', 'ctx'), may hold values from -6 to 6
- gain_attn: bfloat16 [1024], replicated, may hold values from 0.25 to 1.75
- gain_moe: bfloat16 [1024], replicated, may hold values from 0.25 to 1.75
- query_weight: bfloat16 [1024, 1024], P('shard', 'tp'), may hold values from -0.1875 to 0.1875
- key_weight: bfloat16 [1024, 512], P('shard', 'tp'), may hold values from -0.1875 to 0.1875
- value_weight: bfloat16 [1024, 512], P('shard', 'tp'), may hold values from -0.1875 to 0.1875
- out_weight: bfloat16 [1024, 1024], P('tp', 'shard'), may hold values from -3 to 3
- router_weight: bfloat16 [1024, 16], P('shard'), may hold values from -0.09375 to 0.09375
- gate_weight: bfloat16 [16, 1024, 512], P(None, 'shard', 'tp'), may hold values from -0.1875 to 0.1875
- up_weight: bfloat16 [16, 1024, 512], P(None, 'shard', 'tp'), may hold values from -0.1875 to 0.1875
- down_weight: bfloat16 [16, 512, 1024], P(None, 'tp', 'shard'), may hold values from -1 to 1
- expert_routes: int32 [4, 2048, 8], P('shard', 'ctx'), may hold values from 0 to 15, all different within a row; in each aligned block of 512 rows (0 to 511, 512 to 1023, ..., all dimensions but the last counted through in order) at most 320 rows name the same one
- cotangent: bfloat16 [4, 2048, 1024], P('shard', 'ctx'), may hold values from -6 to 6
Outputs:
- output: bfloat16 [4, 2048, 1024], P('shard', 'ctx')
- grad_tokens: bfloat16 [4, 2048, 1024], P('shard', 'ctx')
- grad_gain_attn: float32 [1024], P(('shard', 'ctx'))
- grad_gain_moe: float32 [1024], P(('shard', 'ctx'))
- grad_query_weight: float32 [1024, 1024], P(('shard', 'ctx'), 'tp')
- grad_key_weight: float32 [1024, 512], P(('shard', 'ctx'), 'tp')
- grad_value_weight: float32 [1024, 512], P(('shard', 'ctx'), 'tp')
- grad_out_weight: float32 [1024, 1024], P('tp', ('shard', 'ctx'))
- grad_router_weight: float32 [1024, 16], P(('shard', 'ctx'))
- grad_gate_weight: float32 [16, 1024, 512], P(None, ('shard', 'ctx'), 'tp')
- grad_up_weight: float32 [16, 1024, 512], P(None, ('shard', 'ctx'), 'tp')
- grad_down_weight: float32 [16, 512, 1024], P(None, 'tp', ('shard', 'ctx'))
Inputs may be any that keep to these rules, and one draw needn't show every extreme that they name: `expert_routes`: each row names 8 different experts; in each aligned block of 512 rows of a sequence (the rows of one device) no expert is named by more than 320 rows, a bound that some block reaches.
All inputs are finite; a program needn't handle non-finite values.
Results may differ from a plain program's by a relative error of at most 0.023.
Values may be sent and summed in bfloat16 or wider, within the bound.
A program may use at most 384 MiB of HBM per device.

v0:
```python
import jax
import jax.numpy as jnp
from jax import lax
from jax.sharding import PartitionSpec as P

HD = 64


norm_eps = 1e-06
masked_score = -1e30
precise = lax.Precision.HIGHEST


def rotate(field, positions):
    half_width = field.shape[-1] // 2
    frequency = 10000.0 ** (-2.0 * jnp.arange(half_width, dtype=jnp.float32) / field.shape[-1])
    angles = positions.astype(jnp.float32)[:, None] * frequency[None, :]
    cos_part = jnp.cos(angles)[:, None, :]
    sin_part = jnp.sin(angles)[:, None, :]
    first_half = field[..., :half_width]
    second_half = field[..., half_width:]
    return jnp.concatenate(
        [
            first_half * cos_part - second_half * sin_part,
            second_half * cos_part + first_half * sin_part,
        ],
        axis=-1,
    )


def rotate_back(field, positions):
    half_width = field.shape[-1] // 2
    frequency = 10000.0 ** (-2.0 * jnp.arange(half_width, dtype=jnp.float32) / field.shape[-1])
    angles = positions.astype(jnp.float32)[:, None] * frequency[None, :]
    cos_part = jnp.cos(angles)[:, None, :]
    sin_part = jnp.sin(angles)[:, None, :]
    first_half = field[..., :half_width]
    second_half = field[..., half_width:]
    return jnp.concatenate(
        [
            first_half * cos_part + second_half * sin_part,
            second_half * cos_part - first_half * sin_part,
        ],
        axis=-1,
    )


def rms_scale(field):
    return lax.rsqrt(jnp.mean(field * field, axis=-1, keepdims=True) + norm_eps)


def norm_back(grad_normed, field, row_scale, gain_vec):
    grad_scaled = grad_normed * gain_vec
    grad_field = row_scale * grad_scaled - field * row_scale * row_scale * row_scale * jnp.mean(
        grad_scaled * field, axis=-1, keepdims=True
    )
    grad_gain = jnp.sum(grad_normed * field * row_scale, axis=0)
    return (grad_field, grad_gain)


def expert_work(rows_in, grad_in, gate_in, up_in, down_turned):
    gate_pre = jnp.einsum("ecd,edf->ecf", rows_in, gate_in, preferred_element_type=jnp.float32)
    up_pre = jnp.einsum("ecd,edf->ecf", rows_in, up_in, preferred_element_type=jnp.float32)
    activation = (jax.nn.silu(gate_pre) * up_pre).astype(jnp.bfloat16)
    expert_out = jnp.einsum(
        "ecf,edf->ecd", activation, down_turned, preferred_element_type=jnp.float32
    )
    grad_activation = jnp.einsum(
        "ecd,edf->ecf", grad_in, down_turned, preferred_element_type=jnp.float32
    )
    grad_down_turned = jnp.einsum(
        "ecd,ecf->edf", grad_in, activation, preferred_element_type=jnp.float32
    )
    sigmoid_gate = jax.nn.sigmoid(gate_pre)
    grad_gate_pre = (
        grad_activation * up_pre * sigmoid_gate * (1.0 + gate_pre * (1.0 - sigmoid_gate))
    ).astype(jnp.bfloat16)
    grad_up_pre = (grad_activation * gate_pre * sigmoid_gate).astype(jnp.bfloat16)
    grad_gate_here = jnp.einsum(
        "ecd,ecf->edf", rows_in, grad_gate_pre, preferred_element_type=jnp.float32
    )
    grad_up_here = jnp.einsum(
        "ecd,ecf->edf", rows_in, grad_up_pre, preferred_element_type=jnp.float32
    )
    grad_taken = jnp.einsum(
        "ecf,edf->ecd", grad_gate_pre, gate_in, preferred_element_type=jnp.float32
    ) + jnp.einsum("ecf,edf->ecd", grad_up_pre, up_in, preferred_element_type=jnp.float32)
    return (expert_out, grad_taken, grad_gate_here, grad_up_here, grad_down_turned)


def per_device(
    tokens,
    gain_attn,
    gain_moe,
    query_weight,
    key_weight,
    value_weight,
    out_weight,
    router_weight,
    gate_weight,
    up_weight,
    down_weight,
    expert_routes,
    cotangent,
):
    tok_rows = tokens.shape[1]
    expert_count = gate_weight.shape[0]
    top_count = expert_routes.shape[2]
    capacity = tok_rows * top_count * 5 // (4 * expert_count)
    positions = lax.axis_index("ctx") * tok_rows + jnp.arange(tok_rows)
    full_query, full_key, full_value, full_out, full_router = (
        lax.all_gather(query_weight, "shard", axis=0, tiled=True),
        lax.all_gather(key_weight, "shard", axis=0, tiled=True),
        lax.all_gather(value_weight, "shard", axis=0, tiled=True),
        lax.all_gather(out_weight, "shard", axis=1, tiled=True),
        lax.all_gather(router_weight, "shard", axis=0, tiled=True),
    )
    heads_here = full_query.shape[1] // HD
    kv_here = full_key.shape[1] // HD
    groups = heads_here // kv_here
    score_scale = HD ** (-0.5)
    tok_field = tokens[0].astype(jnp.float32)
    gain_one = gain_attn.astype(jnp.float32)
    gain_two = gain_moe.astype(jnp.float32)
    scale_one = rms_scale(tok_field)
    normed = (tok_field * scale_one * gain_one).astype(jnp.bfloat16)
    queries = rotate(
        jnp.dot(normed, full_query, preferred_element_type=jnp.float32).reshape(
            tok_rows, heads_here, HD
        ),
        positions,
    ).astype(jnp.bfloat16)
    key_rows = rotate(
        jnp.dot(normed, full_key, preferred_element_type=jnp.float32).reshape(
            tok_rows, kv_here, HD
        ),
        positions,
    ).astype(jnp.bfloat16)
    value_rows = (
        jnp.dot(normed, full_value, preferred_element_type=jnp.float32)
        .astype(jnp.bfloat16)
        .reshape(tok_rows, kv_here, HD)
    )
    all_keys, all_values = (
        lax.all_gather(key_rows, "ctx", axis=0, tiled=True),
        lax.all_gather(value_rows, "ctx", axis=0, tiled=True),
    )
    grouped = queries.reshape(tok_rows, kv_here, groups, HD)
    key_pos = jnp.arange(all_keys.shape[0])
    visible = (positions[:, None] >= key_pos[None, :])[None, None]

    def masked_scores():
        raw_scores = (
            jnp.einsum("qgjd,kgd->gjqk", grouped, all_keys, preferred_element_type=jnp.float32)
            * score_scale
        )
        return jnp.where(visible, raw_scores, masked_score)

    scores = masked_scores()
    row_max = jnp.max(scores, axis=-1, keepdims=True)
    exp_vals = jnp.exp(scores - row_max)
    exp_total = jnp.sum(exp_vals, axis=-1, keepdims=True)
    probability_low = (exp_vals / exp_total).astype(jnp.bfloat16)
    log_total = row_max + jnp.log(exp_total)
    attended = (
        jnp.einsum(
            "gjqk,kgd->qgjd", probability_low, all_values, preferred_element_type=jnp.float32
        )
        .reshape(tok_rows, -1)
        .astype(jnp.bfloat16)
    )
    partial_attn = jnp.dot(attended, full_out, preferred_element_type=jnp.float32)
    hidden = tok_field + lax.psum(partial_attn.astype(jnp.bfloat16), "tp").astype(jnp.float32)
    scale_two = rms_scale(hidden)
    normed_moe = (hidden * scale_two * gain_two).astype(jnp.bfloat16)
    logits = jnp.dot(normed_moe, full_router, preferred_element_type=jnp.float32)
    onehot = (expert_routes[0][:, :, None] == jnp.arange(expert_count)[None, None, :]).astype(
        jnp.float32
    )
    chosen = jnp.einsum("tke,te->tk", onehot, logits, precision=precise)
    gating = jax.nn.softmax(chosen, axis=-1)
    flat_hot = onehot.reshape(-1, expert_count)
    before = jnp.cumsum(flat_hot, axis=0) - flat_hot
    rank_of = jnp.sum(before * flat_hot, axis=-1).reshape(tok_rows, top_count)
    slot_hot = (rank_of[:, :, None] == jnp.arange(capacity)[None, None, :]).astype(jnp.float32)
    picked = jnp.einsum("tke,tkc->ect", onehot, slot_hot, precision=precise)
    weighted = jnp.einsum("tke,tkc,tk->ect", onehot, slot_hot, gating, precision=precise)
    taken_rows = jnp.einsum(
        "ect,td->ecd", picked.astype(jnp.bfloat16), normed_moe, preferred_element_type=jnp.float32
    ).astype(jnp.bfloat16)
    grad_out = cotangent[0].astype(jnp.float32)
    grad_expert = jnp.einsum("ect,td->ecd", weighted, grad_out, precision=precise).astype(
        jnp.bfloat16
    )
    down_turned = jnp.swapaxes(down_weight, 1, 2)
    owner_rows, owner_grads, owner_gate, owner_up, owner_down = (
        lax.all_to_all(taken_rows, "shard", split_axis=0, concat_axis=1, tiled=True),
        lax.all_to_all(grad_expert, "shard", split_axis=0, concat_axis=1, tiled=True),
        lax.all_to_all(gate_weight, "shard", split_axis=0, concat_axis=1, tiled=True),
        lax.all_to_all(up_weight, "shard", split_axis=0, concat_axis=1, tiled=True),
        lax.all_to_all(down_turned, "shard", split_axis=0, concat_axis=1, tiled=True),
    )
    owner_results = expert_work(owner_rows, owner_grads, owner_gate, owner_up, owner_down)
    expert_out, grad_taken, grad_gate_rows, grad_up_rows, grad_down_rows = (
        lax.all_to_all(
            owner_results[0].astype(jnp.bfloat16), "shard", split_axis=1, concat_axis=0, tiled=True
        ).astype(jnp.float32),
        lax.all_to_all(
            owner_results[1].astype(jnp.bfloat16), "shard", split_axis=1, concat_axis=0, tiled=True
        ).astype(jnp.float32),
        lax.all_to_all(
            owner_results[2].astype(jnp.bfloat16), "shard", split_axis=1, concat_axis=0, tiled=True
        ).astype(jnp.float32),
        lax.all_to_all(
            owner_results[3].astype(jnp.bfloat16), "shard", split_axis=1, concat_axis=0, tiled=True
        ).astype(jnp.float32),
        lax.all_to_all(
            owner_results[4].astype(jnp.bfloat16), "shard", split_axis=1, concat_axis=0, tiled=True
        ).astype(jnp.float32),
    )
    grad_gate_own, grad_up_own, grad_down_turned = (
        lax.psum_scatter(
            grad_gate_rows.astype(jnp.bfloat16), "ctx", scatter_dimension=1, tiled=True
        ).astype(jnp.float32),
        lax.psum_scatter(
            grad_up_rows.astype(jnp.bfloat16), "ctx", scatter_dimension=1, tiled=True
        ).astype(jnp.float32),
        lax.psum_scatter(
            grad_down_rows.astype(jnp.bfloat16), "ctx", scatter_dimension=1, tiled=True
        ).astype(jnp.float32),
    )
    grad_down_own = jnp.swapaxes(grad_down_turned, 1, 2)
    partial_moe = jnp.einsum("ect,ecd->td", weighted, expert_out, precision=precise)
    result = hidden + lax.psum(partial_moe.astype(jnp.bfloat16), "tp").astype(jnp.float32)
    output = result.astype(jnp.bfloat16)[None]
    slot_products = jnp.einsum("td,ecd->ect", grad_out, expert_out, precision=precise)
    grad_gating_part = jnp.einsum(
        "tke,tkc,ect->tk", onehot, slot_hot, slot_products, precision=precise
    )
    grad_moe_part = jnp.einsum("ect,ecd->td", picked, grad_taken, precision=precise)
    grad_moe_sum, grad_gating = (
        lax.psum(grad_moe_part.astype(jnp.bfloat16), "tp").astype(jnp.float32),
        lax.psum(grad_gating_part.astype(jnp.bfloat16), "tp").astype(jnp.float32),
    )
    grad_chosen = gating * (grad_gating - jnp.sum(gating * grad_gating, axis=-1, keepdims=True))
    grad_logits = jnp.einsum("tke,tk->te", onehot, grad_chosen, precision=precise)
    router_field = full_router.astype(jnp.float32)
    grad_normed_moe = grad_moe_sum + jnp.einsum(
        "te,de->td", grad_logits, router_field, precision=precise
    )
    grad_router_full = jnp.einsum(
        "td,te->de", normed_moe.astype(jnp.float32), grad_logits, precision=precise
    )
    grad_hidden_norm, grad_gain_two = norm_back(grad_normed_moe, hidden, scale_two, gain_two)
    grad_hidden = grad_out + grad_hidden_norm
    grad_branch = grad_hidden.astype(jnp.bfloat16)
    grad_out_full = jnp.einsum(
        "th,td->hd", attended, grad_branch, preferred_element_type=jnp.float32
    )
    grad_attended = (
        jnp.einsum("td,hd->th", grad_branch, full_out, preferred_element_type=jnp.float32)
        .astype(jnp.bfloat16)
        .reshape(tok_rows, kv_here, groups, HD)
    )
    probability_again = jnp.exp(masked_scores() - log_total)
    grad_probability = jnp.einsum(
        "qgjd,kgd->gjqk", grad_attended, all_values, preferred_element_type=jnp.float32
    )
    grad_values_all = jnp.einsum(
        "gjqk,qgjd->kgd",
        probability_again.astype(jnp.bfloat16),
        grad_attended,
        preferred_element_type=jnp.float32,
    )
    inner_sum = jnp.sum(probability_again * grad_probability, axis=-1, keepdims=True)
    grad_scores = (probability_again * (grad_probability - inner_sum)).astype(jnp.bfloat16)
    grad_queries = (
        jnp.einsum("gjqk,kgd->qgjd", grad_scores, all_keys, preferred_element_type=jnp.float32)
        * score_scale
    )
    grad_keys_all = (
        jnp.einsum("gjqk,qgjd->kgd", grad_scores, grouped, preferred_element_type=jnp.float32)
        * score_scale
    )
    grad_keys_own, grad_values_own = (
        lax.psum_scatter(
            grad_keys_all.astype(jnp.bfloat16), "ctx", scatter_dimension=0, tiled=True
        ).astype(jnp.float32),
        lax.psum_scatter(
            grad_values_all.astype(jnp.bfloat16), "ctx", scatter_dimension=0, tiled=True
        ).astype(jnp.float32),
    )
    grad_query_rows = (
        rotate_back(grad_queries.reshape(tok_rows, heads_here, HD), positions)
        .reshape(tok_rows, -1)
        .astype(jnp.bfloat16)
    )
    grad_key_rows = rotate_back(grad_keys_own, positions).reshape(tok_rows, -1).astype(jnp.bfloat16)
    grad_value_rows = grad_values_own.reshape(tok_rows, -1).astype(jnp.bfloat16)
    grad_normed_part = jnp.einsum(
        "th,dh->td", grad_query_rows, full_query, preferred_element_type=jnp.float32
    )
    grad_normed_part = grad_normed_part + jnp.einsum(
        "th,dh->td", grad_key_rows, full_key, preferred_element_type=jnp.float32
    )
    grad_normed_part = grad_normed_part + jnp.einsum(
        "th,dh->td", grad_value_rows, full_value, preferred_element_type=jnp.float32
    )
    grad_query_full = jnp.einsum(
        "td,th->dh", normed, grad_query_rows, preferred_element_type=jnp.float32
    )
    grad_key_full = jnp.einsum(
        "td,th->dh", normed, grad_key_rows, preferred_element_type=jnp.float32
    )
    grad_value_full = jnp.einsum(
        "td,th->dh", normed, grad_value_rows, preferred_element_type=jnp.float32
    )
    grad_normed = lax.psum(grad_normed_part.astype(jnp.bfloat16), "tp").astype(jnp.float32)
    grad_field_norm, grad_gain_one = norm_back(grad_normed, tok_field, scale_one, gain_one)
    grad_tokens = (grad_hidden + grad_field_norm).astype(jnp.bfloat16)[None]
    (
        grad_gain_a,
        grad_gain_m,
        grad_query_own,
        grad_key_own,
        grad_value_own,
        grad_out_own,
        grad_router_own,
    ) = (
        lax.psum_scatter(grad_gain_one, ("shard", "ctx"), scatter_dimension=0, tiled=True),
        lax.psum_scatter(grad_gain_two, ("shard", "ctx"), scatter_dimension=0, tiled=True),
        lax.psum_scatter(grad_query_full, ("shard", "ctx"), scatter_dimension=0, tiled=True),
        lax.psum_scatter(grad_key_full, ("shard", "ctx"), scatter_dimension=0, tiled=True),
        lax.psum_scatter(grad_value_full, ("shard", "ctx"), scatter_dimension=0, tiled=True),
        lax.psum_scatter(grad_out_full, ("shard", "ctx"), scatter_dimension=1, tiled=True),
        lax.psum_scatter(grad_router_full, ("shard", "ctx"), scatter_dimension=0, tiled=True),
    )
    return (
        output,
        grad_tokens,
        grad_gain_a,
        grad_gain_m,
        grad_query_own,
        grad_key_own,
        grad_value_own,
        grad_out_own,
        grad_router_own,
        grad_gate_own,
        grad_up_own,
        grad_down_own,
    )


def solution(mesh):
    placed = (
        P("shard", "ctx", None),
        P(),
        P(),
        P("shard", "tp"),
        P("shard", "tp"),
        P("shard", "tp"),
        P("tp", "shard"),
        P("shard", None),
        P(None, "shard", "tp"),
        P(None, "shard", "tp"),
        P(None, "tp", "shard"),
        P("shard", "ctx", None),
        P("shard", "ctx", None),
    )
    return jax.shard_map(
        per_device,
        mesh=mesh,
        in_specs=placed,
        out_specs=(
            P("shard", "ctx", None),
            P("shard", "ctx", None),
            P(("shard", "ctx")),
            P(("shard", "ctx")),
            P(("shard", "ctx"), "tp"),
            P(("shard", "ctx"), "tp"),
            P(("shard", "ctx"), "tp"),
            P("tp", ("shard", "ctx")),
            P(("shard", "ctx"), None),
            P(None, ("shard", "ctx"), "tp"),
            P(None, ("shard", "ctx"), "tp"),
            P(None, "tp", ("shard", "ctx")),
        ),
        check_vma=False,
    )
```

profile of v0, /device:TPU:0, one launch (start us, length us, event | category | flops | bytes accessed | tf_op | source)
XLA Modules:
  0.0 1608.7 jit_solution(16023405395768566415)
XLA Ops:
  8.0 8.9 all_gather.23
  19.9 10.4 all_gather.21
  41.5 8.3 reduce-window.6
  55.3 6.7 all-gather.7.cloned.1.call-done
  62.0 15.1 fusion.114
  77.1 13.1 fusion.3
  91.0 14.9 fusion.63
  105.9 4.5 all-to-all-start.2
  117.1 7.0 fusion.13
  124.0 12.0 copy.113
  136.1 17.9 %all-reduce.8.cloned.1.call-done = bf16[512,1024]{1,0:T(8,128)(2,1)} async-done(((bf16[512,1024]{1,0:T(8,128)(2,1)}), bf16[512,1024]{1,0:T(8,128)(2,1)}) %all-reduce.8.cloned.1.call-update) | async-done | bytes 1048592 | tf_op jit(solution)/shard_map/psum | solution.py:173
  155.6 4.6 all-to-all-start.3
  161.7 12.1 convolution_convert_fusion.2
  173.8 12.2 all-to-all-done.3
  186.0 6.3 all-to-all-start
  195.6 4.1 copy.117
  199.8 108.2 %all-to-all-done = bf16[16,320,1024]{2,1,0:T(8,128)(2,1)} async-done(((bf16[16,320,1024]{2,1,0:T(8,128)(2,1)}), bf16[16,320,1024]{2,1,0:T(8,128)(2,1)}, u32[]{:S(2)}, u32[]{:S(2)}) %all-to-all-start) | async-done | bytes 10485792 | tf_op jit(solution)/shard_map/all_to_all | solution.py:197
  308.0 9.5 copy.114
  317.5 9.9 fusion.118
  327.4 7.5 multiply_convert_fusion.2
  334.9 5.3 convolution_convert_fusion
  340.2 28.3 %copy.118 = bf16[4,1280,1024]{2,0,1:T(4,128)(2,1)} copy(bf16[4,1280,1024]{2,1,0:T(8,128)(2,1)S(1)} %convolution_convert_fusion) | data formatting | bytes 20971520 | tf_op jit(solution)/shard_map/convert_element_type | solution.py:206
  368.5 6.3 all-to-all-start.4
  374.8 116.6 %all_gather.27 = bf16[1024,16]{0,1:T(8,128)(2,1)S(1)} all-gather(bf16[256,16]{0,1:T(8,128)(2,1)S(1)} %copy-done.47), channel_id=1, replica_groups=mesh['shard'=4,'ctx'=4,'tp'=2] {'shard'}, dimensions={0}, use_global_device_ids=true | all-gather | bytes 40960 | tf_op jit(solution)/shard_map/all_gather | solution.py:116
  496.3 11.9 copy.119
  508.2 10.9 fusion.72
  519.2 12.2 copy.125
  531.3 13.9 select_reduce_fusion
  545.2 8.5 psum.38
  554.1 10.4 fusion.16
  564.5 12.0 copy.120
  576.5 19.3 %convolution_convert_fusion.1 = bf16[16,320,1024]{2,1,0:T(8,128)(2,1)S(1)} fusion(f32[16,320,512]{2,1,0:T(8,128)} %copy.120, bf16[1,512,1024]{2,1,0:T(8,128)(2,1)} %param.25), kind=kOutput, calls=%fused_computation.24 | convolution fusion | flops 32217497600 | bytes 22020096 | tf_op jit(solution)/shard_map/ect,td->ecd/dot_general | solution.py:192
  595.8 119.9 %all_to_all.180 = bf16[16,320,1024]{2,1,0:T(8,128)(2,1)} all-to-all(bf16[16,320,1024]{2,1,0:T(8,128)(2,1)S(1)} %convolution_convert_fusion.1), channel_id=1, replica_groups=mesh['shard'=4,'ctx'=4,'tp'=2] {'shard'}, dimensions={0} | all-to-all | bytes 20971520 | tf_op jit(solution)/shard_map/all_to_all | solution.py:198
  715.7 9.6 copy.122
  725.3 13.9 multiply_convert_fusion
  739.2 8.6 fusion.119
  747.8 12.9 add_convert_fusion
  760.7 12.3 copy.123
  773.0 119.6 %all_to_all.181 = bf16[4,1280,1024]{2,0,1:T(4,128)(2,1)} all-to-all(bf16[4,1280,1024]{2,0,1:T(4,128)(2,1)S(1)} %copy.123), channel_id=1, replica_groups=mesh['shard'=4,'ctx'=4,'tp'=2] {'shard'}, dimensions={1} | all-to-all | bytes 20971520 | tf_op jit(solution)/shard_map/all_to_all | solution.py:208
  892.7 11.8 copy.124
  904.5 20.8 %bitcast_convert_fusion.2 = bf16[512,1024]{1,0:T(8,128)(2,1)} fusion(bf16[16,320,1024]{2,1,0:T(8,128)(2,1)} %bitcast.313, f32[512,320,16]{0,1,2:T(8,128)} %copy.113), kind=kOutput, calls=%fused_computation.72 | convolution fusion | flops 32212779008 | bytes 22020096 | tf_op jit(solution)/shard_map/ect,ecd->td/dot_general | solution.py:240
  928.7 37.1 %all-reduce.10.cloned.1.call-done = bf16[512,1024]{1,0:T(8,128)(2,1)} async-done(((bf16[512,1024]{1,0:T(8,128)(2,1)}), bf16[512,1024]{1,0:T(8,128)(2,1)}) %all-reduce.10.cloned.1.call-update) | async-done | bytes 1048592 | tf_op jit(solution)/shard_map/psum | solution.py:242
  971.4 21.6 %fusion = (f32[4,2,512]{2,1,0:T(2,128)S(1)}, f32[4,2048,512,2]{2,1,3,0:T(8,128)}) fusion(f32[4,2,512,2048]{2,3,1,0:T(8,128)} %get-tuple-element.37, f32[4,2,512]{2,1,0:T(2,128)S(1)} %bitcast.351, bf16[512,4,2,64]{0,3,2,1:T(8,128)(2,1)S(1)} %bitcast.322, bf16[2048,4,64]{0,2,1:T(8,128)(2,1)S(1)} %copy-done.26), kind=kOutput, calls=%fused_computation.2 | convolution fusion | flops 1098903552 | bytes 68714496 | tf_op jit(solution)/shard_map/qgjd,kgd->gjqk/dot_general | solution.py:266
  993.0 27.7 %fusion.2 = bf16[4,2,512,2048]{2,3,1,0:T(8,128)(2,1)} fusion(f32[4,2048,512,2]{2,1,3,0:T(8,128)} %get-tuple-element.42, f32[4,2,512,2048]{2,3,1,0:T(8,128)} %get-tuple-element.37, f32[4,2,512]{2,1,0:T(2,128)S(1)} %get-tuple-element.41, f32[4,2,512]{2,1,0:T(2,128)S(1)} %bitcast.352), kind=kLoop, calls=%fused_computation.4 | loop fusion | flops 33554432 | bytes 83918848 | tf_op jit(solution)/shard_map/convert_element_type | solution.py:276
  1020.8 12.0 fusion.44
  1032.8 15.0 fusion.41
  1047.9 9.8 convolution_convert_fusion.5
  1057.6 4.6 copy.130
  1062.2 4.6 all-to-all-start.7
  1070.3 22.3 %all-to-all-done.7 = bf16[4,1024,256]{2,0,1:T(4,128)(2,1)} async-done(((bf16[4,1024,256]{2,0,1:T(4,128)(2,1)}), bf16[4,1024,256]{2,0,1:T(4,128)(2,1)}, u32[]{:S(2)}, u32[]{:S(2)}) %all-to-all-start.7) | async-done | bytes 2097184 | tf_op jit(solution)/shard_map/all_to_all | solution.py:211
  1096.1 9.8 convolution_convert_fusion.4
  1109.1 29.9 %all_to_all.182 = bf16[4,1024,256]{2,0,1:T(4,128)(2,1)S(1)} all-to-all(bf16[4,1024,256]{2,0,1:T(4,128)(2,1)S(1)} %copy.133), channel_id=1, replica_groups=mesh['shard'=4,'ctx'=4,'tp'=2] {'shard'}, dimensions={1} | all-to-all | bytes 4194304 | tf_op jit(solution)/shard_map/all_to_all | solution.py:214
  1140.8 9.8 convolution_convert_fusion.3
  1153.7 28.2 %all_to_all.183 = bf16[4,1024,256]{2,0,1:T(4,128)(2,1)S(1)} all-to-all(bf16[4,1024,256]{2,0,1:T(4,128)(2,1)S(1)} %copy.136), channel_id=1, replica_groups=mesh['shard'=4,'ctx'=4,'tp'=2] {'shard'}, dimensions={1} | all-to-all | bytes 4194304 | tf_op jit(solution)/shard_map/all_to_all | solution.py:217
  1183.9 20.9 %bitcast_convert_fusion.3 = bf16[512,1024]{1,0:T(8,128)(2,1)} fusion(f32[16,320,512]{2,1,0:T(8,128)} %copy.120, bf16[16,320,1024]{2,1,0:T(8,128)(2,1)} %bitcast.306), kind=kOutput, calls=%fused_computation.73 | convolution fusion | flops 32212779008 | bytes 22020096 | tf_op jit(solution)/shard_map/ect,ecd->td/dot_general | solution.py:233
  1204.8 8.7 convolution_multiply_fusion
  1243.2 40.9 %reduce-scatter.29.cloned.1.call-done = bf16[16,64,256]{2,1,0:T(8,128)(2,1)} async-done(((bf16[16,256,256]{2,1,0:T(8,128)(2,1)}), bf16[16,64,256]{2,1,0:T(8,128)(2,1)}) %reduce-scatter.29.cloned.1.call-update) | async-done | bytes 524304 | tf_op jit(solution)/shard_map/reduce_scatter | solution.py:228
  1286.2 63.3 %all-reduce.12.cloned.1.call-done = (bf16[512,1024]{1,0:T(8,128)(2,1)}, bf16[512,1024]{1,0:T(8,128)(2,1)}) async-done(((bf16[512,1024]{1,0:T(8,128)(2,1)}, bf16[512,1024]{1,0:T(8,128)(2,1)}), (bf16[512,1024]{1,0:T(8,128)(2,1)}, bf16[512,1024]{1,0:T(8,128)(2,1)})) %all-reduce.12.cloned.1.call-update) | async-done | bytes 2097168 | tf_op jit(solution)/shard_map/psum | solution.py:234
  1351.5 34.1 %all-reduce.2 = (f32[1024]{0:T(1024)S(1)}, f32[1024]{0:T(1024)S(1)}) all-reduce(f32[1024]{0:T(1024)S(1)} %get-tuple-element.14, f32[1024]{0:T(1024)S(1)} %get-tuple-element.12), channel_id=4, replica_groups=mesh['shard'=4,'ctx'=4,'tp'=2] {'shard','ctx'}, use_global_device_ids=true, to_apply=%region_21.22.clone | all-reduce | flops 2048 | bytes 16384
  1386.8 4.2 fusion.65
  1391.1 24.6 %reduce-scatter.23.cloned.1.call-done = f32[512,64]{0,1:T(8,128)} async-done(((f32[512,1024]{0,1:T(8,128)}), f32[512,64]{0,1:T(8,128)}) %reduce-scatter.23.cloned.1.call-update) | async-done | bytes 131088 | tf_op jit(solution)/shard_map/reduce_scatter | solution.py:335
  1415.7 64.7 %reduce-scatter.17.cloned.1.call-done = f32[64,512]{1,0:T(8,128)} async-done(((f32[1024,512]{1,0:T(8,128)}), f32[64,512]{1,0:T(8,128)}) %reduce-scatter.17.cloned.1.call-update) | async-done | bytes 131088 | tf_op jit(solution)/shard_map/reduce_scatter | solution.py:332
  1480.4 60.8 %reduce-scatter.21.cloned.1.call-done = f32[64,256]{1,0:T(8,128)} async-done(((f32[1024,256]{1,0:T(8,128)}), f32[64,256]{1,0:T(8,128)}) %reduce-scatter.21.cloned.1.call-update) | async-done | bytes 65552 | tf_op jit(solution)/shard_map/reduce_scatter | solution.py:334
  1541.2 60.5 %reduce-scatter.19.cloned.1.call-done = f32[64,256]{1,0:T(8,128)} async-done(((f32[1024,256]{1,0:T(8,128)}), f32[64,256]{1,0:T(8,128)}) %reduce-scatter.19.cloned.1.call-update) | async-done | bytes 65552 | tf_op jit(solution)/shard_map/reduce_scatter | solution.py:333
  (219 shorter events, 99.3 us)
Async XLA Ops:
  7.2 10.6 copy-start
  7.2 42.7 %all-gather.9.cloned.1.call-start = ((), (), s32[]{:S(2)}) async-start(), calls=%async_computation.22 | async-start | bytes 1310720 | tf_op jit(solution)/shard_map/all_gather | solution.py:112
  7.9 54.0 %all-gather.7.cloned.1.call-start = ((), (), s32[]{:S(2)}) async-start(), calls=%async_computation.21 | async-start | bytes 1310720 | tf_op jit(solution)/shard_map/all_gather | solution.py:145
  17.5 34.7 %copy-start.38 = (f32[1024]{0:T(1024)}, f32[1024]{0:T(1024)S(1)}, u32[]{:S(2)}) copy-start(f32[1024]{0:T(1024)S(1)} %convert_element_type.229) | copy-start | bytes 12292
  18.1 34.2 %copy-start.43 = (f32[512]{0:T(512)}, f32[512]{0:T(512)S(1)}, u32[]{:S(2)}) copy-start(f32[512]{0:T(512)S(1)} %add_rsqrt_fusion.1) | copy-start | bytes 6148
  18.4 35.9 %copy-start.22 = (f32[512,32]{0,1:T(8,128)}, f32[512,32]{0,1:T(8,128)S(1)}, u32[]{:S(2)}) copy-start(f32[512,32]{0,1:T(8,128)S(1)} %get-tuple-element.34) | copy-start | bytes 196612
  18.4 35.9 %copy-start.24 = (f32[512,32]{0,1:T(8,128)}, f32[512,32]{0,1:T(8,128)S(1)}, u32[]{:S(2)}) copy-start(f32[512,32]{0,1:T(8,128)S(1)} %get-tuple-element.35) | copy-start | bytes 196612
  19.8 71.2 %all-gather.5.cloned.1.call-start = ((), (), s32[]{:S(2)}) async-start(), calls=%async_computation.20 | async-start | bytes 1310720 | tf_op jit(solution)/shard_map/all_gather | solution.py:146
  32.5 73.5 %all-to-all-start.1 = ((bf16[16,256,256]{2,1,0:T(8,128)(2,1)}), bf16[16,256,256]{2,1,0:T(8,128)(2,1)S(1)}, u32[]{:S(2)}, u32[]{:S(2)}) async-start(bf16[16,256,256]{2,1,0:T(8,128)(2,1)} %param.21), calls=%async_computation.1 | async-start | bytes 4194304 | tf_op jit(solution)/shard_map/all_to_all | solution.py:199
  36.1 74.6 %all-gather.11.cloned.1.call-start = ((), (), s32[]{:S(2)}) async-start(), calls=%async_computation.23 | async-start | bytes 1310720 | tf_op jit(solution)/shard_map/all_gather | solution.py:115
  37.5 2.2 copy-start.20
  49.8 64.0 %copy-start.19 = (f32[16,32,128]{2,1,0:T(8,128)}, f32[16,32,128]{2,1,0:T(8,128)S(1)}, u32[]{:S(2)}) copy-start(f32[16,32,128]{2,1,0:T(8,128)S(1)} %reduce-window.6) | copy-start | bytes 786436
  77.1 13.9 copy-start.34
  90.3 15.7 copy-start.36
  105.9 7.9 copy-start.8
  105.9 49.7 %all-to-all-start.2 = ((bf16[16,256,256]{2,1,0:T(8,128)(2,1)}), bf16[16,256,256]{2,1,0:T(8,128)(2,1)}, u32[]{:S(2)}, u32[]{:S(2)}) async-start(bf16[16,256,256]{2,1,0:T(8,128)(2,1)} %param.22), calls=%async_computation.2 | async-start | bytes 4194304 | tf_op jit(solution)/shard_map/all_to_all | solution.py:200
  110.4 4.8 copy-start.48
  110.4 4.8 copy-start.42
  110.4 43.5 %all-reduce.8.cloned.1.call-start = ((), (), s32[]{:S(2)}) async-start(), calls=%async_computation.24 | async-start | bytes 2097152 | tf_op jit(solution)/shard_map/psum | solution.py:173
  115.2 45.0 %copy-start.40 = (f32[1024]{0:T(1024)}, f32[1024]{0:T(1024)S(1)}, u32[]{:S(2)}) copy-start(f32[1024]{0:T(1024)S(1)} %convert_element_type.245) | copy-start | bytes 12292
  117.0 7.0 copy-start.10
  155.6 4.7 copy-start.2
  155.6 30.4 %all-to-all-start.3 = ((bf16[16,256,256]{1,2,0:T(8,128)(2,1)}), bf16[16,256,256]{1,2,0:T(8,128)(2,1)}, u32[]{:S(2)}, u32[]{:S(2)}) async-start(bf16[16,256,256]{1,2,0:T(8,128)(2,1)} %bitcast.332), calls=%async_computation.3 | async-start | bytes 4194304 | tf_op jit(solution)/shard_map/all_to_all | solution.py:201
  160.3 13.5 copy-start.45
  173.8 18.6 %copy-start.9 = (bf16[16,256,256]{2,1,0:T(8,128)(2,1)S(1)}, bf16[16,256,256]{2,1,0:T(8,128)(2,1)}, u32[]{:S(2)}) copy-start(bf16[16,256,256]{2,1,0:T(8,128)(2,1)} %copy-done.8) | copy-start | bytes 6291460
  186.0 122.0 %all-to-all-start = ((bf16[16,320,1024]{2,1,0:T(8,128)(2,1)}), bf16[16,320,1024]{2,1,0:T(8,128)(2,1)}, u32[]{:S(2)}, u32[]{:S(2)}) async-start(bf16[16,320,1024]{2,1,0:T(8,128)(2,1)} %convolution_convert_fusion.2), calls=%async_computation | async-start | bytes 20971520 | tf_op jit(solution)/shard_map/all_to_all | solution.py:197
  317.5 9.9 copy-start.5
  368.5 6.3 copy-start.47
  368.5 127.8 %all-to-all-start.4 = ((bf16[4,1280,1024]{2,0,1:T(4,128)(2,1)}), bf16[4,1280,1024]{2,0,1:T(4,128)(2,1)}, u32[]{:S(2)}, u32[]{:S(2)}) async-start(bf16[4,1280,1024]{2,0,1:T(4,128)(2,1)} %copy.118), calls=%async_computation.4 | async-start | bytes 20971520 | tf_op jit(solution)/shard_map/all_to_all | solution.py:205
  374.8 591.0 %all-reduce.10.cloned.1.call-start = ((), (), s32[]{:S(2)}) async-start(), calls=%async_computation.25 | async-start | bytes 2097152 | tf_op jit(solution)/shard_map/psum | solution.py:242
  519.2 12.2 copy-start.11
  554.0 10.4 copy-start.16
  725.3 13.9 copy-start.7
  739.2 8.6 copy-start.18
  904.5 20.9 %copy-start.35 = (f32[4,2,512]{2,1,0:T(2,128)S(1)}, f32[4,2,512]{2,1,0:T(2,128)}, u32[]{:S(2)}) copy-start(f32[4,2,512]{2,1,0:T(2,128)} %copy-done.34) | copy-start | bytes 49156
  904.5 20.9 %copy-start.37 = (f32[4,2,512]{2,1,0:T(2,128)S(1)}, f32[4,2,512]{2,1,0:T(2,128)}, u32[]{:S(2)}) copy-start(f32[4,2,512]{2,1,0:T(2,128)} %copy-done.36) | copy-start | bytes 49156
  904.5 21.0 %copy-start.17 = (f32[512,8]{1,0:T(8,128)S(1)}, f32[512,8]{1,0:T(8,128)}, u32[]{:S(2)}) copy-start(f32[512,8]{1,0:T(8,128)} %copy-done.16) | copy-start | bytes 49156
  925.3 40.5 %copy-start.1 = (bf16[1,512,1024]{2,1,0:T(8,128)(2,1)S(1)}, bf16[1,512,1024]{2,1,0:T(8,128)(2,1)}, u32[]{:S(2)}) copy-start(bf16[1,512,1024]{2,1,0:T(8,128)(2,1)} %param.13) | copy-start | bytes 3145732
  925.3 40.5 %copy-start.3 = (bf16[512,1024]{1,0:T(8,128)(2,1)S(1)}, bf16[512,1024]{1,0:T(8,128)(2,1)}, u32[]{:S(2)}) copy-start(bf16[512,1024]{1,0:T(8,128)(2,1)} %all-reduce.8.cloned.1.call-done) | copy-start | bytes 3145732
  925.3 40.5 %copy-start.41 = (f32[1024]{0:T(1024)S(1)}, f32[1024]{0:T(1024)}, u32[]{:S(2)}) copy-start(f32[1024]{0:T(1024)} %copy-done.40) | copy-start | bytes 12292
  925.3 40.5 %copy-start.46 = (f32[512]{0:T(512)S(1)}, f32[512]{0:T(512)}, u32[]{:S(2)}) copy-start(f32[512]{0:T(512)} %copy-done.45) | copy-start | bytes 6148
  925.4 291.7 %reduce-scatter.13.cloned.1.call-start = ((), (), s32[]{:S(2)}) async-start(), calls=%async_computation.26 | async-start | bytes 1310720 | tf_op jit(solution)/shard_map/reduce_scatter | solution.py:286
  928.7 40.2 %copy-start.30 = (f32[512,1,16]{2,1,0:T(1,128)}, f32[512,1,16]{2,1,0:T(1,128)S(1)}, u32[]{:S(2)}) copy-start(f32[512,1,16]{2,1,0:T(1,128)S(1)} %fusion.57) | copy-start | bytes 98308
  965.8 3.1 copy-start.4
  965.8 3.1 copy-start.32
  970.9 22.1 %copy-start.12 = (bf16[512,512]{0,1:T(8,128)(2,1)}, bf16[512,512]{0,1:T(8,128)(2,1)S(1)}, u32[]{:S(2)}) copy-start(bf16[512,512]{0,1:T(8,128)(2,1)S(1)} %convolution_convert_fusion.7) | copy-start | bytes 1572868
  993.0 27.8 %copy-start.27 = (bf16[512,8,32]{0,2,1:T(8,128)(2,1)S(1)}, bf16[512,8,32]{0,2,1:T(8,128)(2,1)}, u32[]{:S(2)}) copy-start(bf16[512,8,32]{0,2,1:T(8,128)(2,1)} %get-tuple-element.26) | copy-start | bytes 786436
  1032.8 188.3 %reduce-scatter.15.cloned.1.call-start = ((), (), s32[]{:S(2)}) async-start(), calls=%async_computation.27 | async-start | bytes 1310720 | tf_op jit(solution)/shard_map/reduce_scatter | solution.py:289
  1062.2 4.7 copy-start.31
  1062.2 30.4 %all-to-all-start.7 = ((bf16[4,1024,256]{2,0,1:T(4,128)(2,1)}), bf16[4,1024,256]{2,0,1:T(4,128)(2,1)}, u32[]{:S(2)}, u32[]{:S(2)}) async-start(bf16[4,1024,256]{2,0,1:T(4,128)(2,1)} %copy.130), calls=%async_computation.13 | async-start | bytes 4194304 | tf_op jit(solution)/shard_map/all_to_all | solution.py:211
  1066.8 170.7 %reduce-scatter.31.cloned.1.call-start = ((), (), s32[]{:S(2)}) async-start(), calls=%async_computation.35 | async-start | bytes 557056
  1070.2 168.7 %reduce-scatter.25.cloned.1.call-start = ((), (), s32[]{:S(2)}) async-start(), calls=%async_computation.32 | async-start | bytes 2621440 | tf_op jit(solution)/shard_map/reduce_scatter | solution.py:222
  1095.9 145.2 %reduce-scatter.27.cloned.1.call-start = ((), (), s32[]{:S(2)}) async-start(), calls=%async_computation.33 | async-start | bytes 2621440 | tf_op jit(solution)/shard_map/reduce_scatter | solution.py:225
  1140.7 143.3 %reduce-scatter.29.cloned.1.call-start = ((), (), s32[]{:S(2)}) async-start(), calls=%async_computation.34 | async-start | bytes 2621440 | tf_op jit(solution)/shard_map/reduce_scatter | solution.py:228
  1183.7 165.8 %all-reduce.12.cloned.1.call-start = ((), (), s32[]{:S(2)}) async-start(), calls=%async_computation.36 | async-start | bytes 4194304 | tf_op jit(solution)/shard_map/psum | solution.py:234
  1183.9 20.9 %copy-start.28 = (bf16[2048,4,64]{0,2,1:T(8,128)(2,1)S(1)}, bf16[2048,4,64]{0,2,1:T(8,128)(2,1)}, u32[]{:S(2)}) copy-start(bf16[2048,4,64]{0,2,1:T(8,128)(2,1)} %all-gather.7.cloned.1.call-done) | copy-start | bytes 3145732
  1204.8 8.8 copy-start.23
  1204.8 8.8 copy-start.25
  1225.0 3.3 copy-start.39
  1225.1 3.3 copy-start.44
  1225.1 190.6 %reduce-scatter.23.cloned.1.call-start = ((), (), s32[]{:S(2)}) async-start(), calls=%async_computation.31 | async-start | bytes 2228224 | tf_op jit(solution)/shard_map/reduce_scatter | solution.py:335
  1228.3 252.1 %reduce-scatter.17.cloned.1.call-start = ((), (), s32[]{:S(2)}) async-start(), calls=%async_computation.28 | async-start | bytes 2228224 | tf_op jit(solution)/shard_map/reduce_scatter | solution.py:332
  1231.7 309.5 %reduce-scatter.21.cloned.1.call-start = ((), (), s32[]{:S(2)}) async-start(), calls=%async_computation.30 | async-start | bytes 1114112 | tf_op jit(solution)/shard_map/reduce_scatter | solution.py:334
  1234.3 367.4 %reduce-scatter.19.cloned.1.call-start = ((), (), s32[]{:S(2)}) async-start(), calls=%async_computation.29 | async-start | bytes 1114112 | tf_op jit(solution)/shard_map/reduce_scatter | solution.py:333
  (9 other events, 11.9 us)
Sparse Core Ops, SparseCore 0:
  9.6 22.2 all-gather.8
  34.0 27.9 all-gather.6
  63.5 27.4 all-gather.4
  92.4 16.3 all-gather.10
  114.0 39.9 all-reduce.7
  925.5 40.2 all-reduce.9
  1032.9 27.1 reduce-scatter.12
  1063.0 25.7 reduce-scatter.14
  1092.4 55.3 reduce-scatter.30
  1150.1 42.8 reduce-scatter.24
  1195.3 43.1 reduce-scatter.26
  1240.8 43.1 reduce-scatter.28
  1287.0 62.4 all-reduce.11
  1354.1 61.5 reduce-scatter.22
  1419.8 60.5 reduce-scatter.16
  1484.9 56.2 reduce-scatter.20
  1545.3 56.4 reduce-scatter.18
where the time goes:
time: 1620 us; the launch traced here: 1610 us
  waiting for transfers between devices  521 us (32%)
  blocking collectives  476 us (29%)
  matrix products  331 us (20%)
  local copies, waits for them, and re-layouts  158 us (10%)
  other arithmetic  74.8 us (5%)
  starting transfers between devices  31.5 us (2%)
    all_to_all x1, blocking collectives, per_device(): lax.all_to_all(grad_expert, 'shard', split_axis=0, concat_axis=1, tiled=T...  120 us
    all_to_all x1, blocking collectives, per_device(): lax.all_to_all(owner_results[1].astype(jnp.bfloat16), 'shard', split_axis...  120 us
    all_gather x1, blocking collectives, per_device(): lax.all_gather(router_weight, 'shard', axis=0, tiled=True)  117 us
    all_to_all x1, waiting for transfers between devices, per_device(): lax.all_to_all(taken_rows, 'shard', split_axis=0, concat_axis=1, tiled=True)  108 us
    reduce_scatter x1, waiting for transfers between devices, per_device(): lax.psum_scatter(grad_query_full, ('shard', 'ctx'), scatter_dimension=0,...  64.7 us
    psum x1, waiting for transfers between devices, per_device(): lax.psum(partial_moe.astype(jnp.bfloat16), 'tp').astype(jnp.float32)  63.3 us
    reduce_scatter x1, waiting for transfers between devices, per_device(): lax.psum_scatter(grad_value_full, ('shard', 'ctx'), scatter_dimension=0,...  60.8 us
    reduce_scatter x1, waiting for transfers between devices, per_device(): lax.psum_scatter(grad_key_full, ('shard', 'ctx'), scatter_dimension=0, ti...  60.5 us
  transfers between devices with their start and end apart: 23, of which 13 were waited for; matrix products, arithmetic and copies ran while one was open for 16% of the time, Pallas kernels for 0%

commit v1 on v0

v1 whole, which is shorter than its diff:
```python
import jax
import jax.numpy as jnp
from jax import lax
from jax.sharding import PartitionSpec as P

HD = 64


norm_eps = 1e-06
masked_score = -1e30
precise = lax.Precision.HIGHEST


def rotate(field, positions):
    half_width = field.shape[-1] // 2
    frequency = 10000.0 ** (-2.0 * jnp.arange(half_width, dtype=jnp.float32) / field.shape[-1])
    angles = positions.astype(jnp.float32)[:, None] * frequency[None, :]
    cos_part = jnp.cos(angles)[:, None, :]
    sin_part = jnp.sin(angles)[:, None, :]
    first_half = field[..., :half_width]
    second_half = field[..., half_width:]
    return jnp.concatenate(
        [
            first_half * cos_part - second_half * sin_part,
            second_half * cos_part + first_half * sin_part,
        ],
        axis=-1,
    )


def rotate_back(field, positions):
    half_width = field.shape[-1] // 2
    frequency = 10000.0 ** (-2.0 * jnp.arange(half_width, dtype=jnp.float32) / field.shape[-1])
    angles = positions.astype(jnp.float32)[:, None] * frequency[None, :]
    cos_part = jnp.cos(angles)[:, None, :]
    sin_part = jnp.sin(angles)[:, None, :]
    first_half = field[..., :half_width]
    second_half = field[..., half_width:]
    return jnp.concatenate(
        [
            first_half * cos_part + second_half * sin_part,
            second_half * cos_part - first_half * sin_part,
        ],
        axis=-1,
    )


def rms_scale(field):
    return lax.rsqrt(jnp.mean(field * field, axis=-1, keepdims=True) + norm_eps)


def norm_back(grad_normed, field, row_scale, gain_vec):
    grad_scaled = grad_normed * gain_vec
    grad_field = row_scale * grad_scaled - field * row_scale * row_scale * row_scale * jnp.mean(
        grad_scaled * field, axis=-1, keepdims=True
    )
    grad_gain = jnp.sum(grad_normed * field * row_scale, axis=0)
    return (grad_field, grad_gain)


def swap_tp(part):
    return lax.ppermute(part, "tp", [(0, 1), (1, 0)])


def sum_tp(part):
    low = part.astype(jnp.bfloat16)
    return low.astype(jnp.float32) + swap_tp(low).astype(jnp.float32)


def scatter_sum(grad, rows):
    parts = lax.psum_scatter(
        grad.reshape(lax.axis_size("shard"), lax.axis_size("ctx"), rows, grad.shape[1]),
        "shard",
        scatter_dimension=0,
        tiled=False,
    )
    return lax.psum_scatter(parts, "ctx", scatter_dimension=0, tiled=False)


def per_device(
    tokens,
    gain_attn,
    gain_moe,
    query_weight,
    key_weight,
    value_weight,
    out_weight,
    router_weight,
    gate_weight,
    up_weight,
    down_weight,
    expert_routes,
    cotangent,
):
    shards = lax.axis_size("shard")
    ctxs = lax.axis_size("ctx")
    shard_at = lax.axis_index("shard")
    ctx_at = lax.axis_index("ctx")
    tok_rows = tokens.shape[1]
    width = tokens.shape[2]
    expert_count = gate_weight.shape[0]
    own = expert_count // shards
    hidden_here = gate_weight.shape[2]
    width_here = gate_weight.shape[1]
    own_rows = width // (shards * ctxs)
    span = own * hidden_here
    positions = ctx_at * tok_rows + jnp.arange(tok_rows)

    q_cols = query_weight.shape[1]
    k_cols = key_weight.shape[1]
    full_qkv = lax.all_gather(
        jnp.concatenate([query_weight, key_weight, value_weight], axis=1),
        "shard", axis=0, tiled=True,
    )
    full_out = lax.all_gather(out_weight.T, "shard", axis=0, tiled=True)
    full_router = lax.all_gather(router_weight, "shard", axis=0, tiled=True)

    stacked = jnp.stack([gate_weight, up_weight, jnp.swapaxes(down_weight, 1, 2)], axis=0)
    stacked = stacked.reshape(3, shards, own, width_here, hidden_here).transpose(1, 3, 0, 2, 4)
    stacked = stacked.reshape(shards, width_here, 3 * span)
    expert_weights = lax.all_to_all(
        stacked, "shard", split_axis=0, concat_axis=0, tiled=True
    ).reshape(width, 3 * span)
    weight_gu = expert_weights[:, : 2 * span]
    weight_down = expert_weights[:, 2 * span :]
    chosen_here = jnp.sum(
        (expert_routes[0][:, :, None] == jnp.arange(expert_count)[None, None, :]).astype(
            jnp.float32
        ),
        axis=1,
    )
    chosen_all = lax.all_gather(chosen_here.astype(jnp.bfloat16), "shard", axis=0, tiled=True)
    cot_all = lax.all_gather(cotangent[0], "shard", axis=0, tiled=True)

    heads_here = q_cols // HD
    kv_here = k_cols // HD
    groups = heads_here // kv_here
    score_scale = HD ** (-0.5)
    tok_field = tokens[0].astype(jnp.float32)
    gain_one = gain_attn.astype(jnp.float32)
    gain_two = gain_moe.astype(jnp.float32)
    scale_one = rms_scale(tok_field)
    normed = (tok_field * scale_one * gain_one).astype(jnp.bfloat16)
    projected = jnp.dot(normed, full_qkv, preferred_element_type=jnp.float32)
    queries = rotate(
        projected[:, :q_cols].reshape(tok_rows, heads_here, HD), positions
    ).astype(jnp.bfloat16)
    key_rows = rotate(
        projected[:, q_cols : q_cols + k_cols].reshape(tok_rows, kv_here, HD), positions
    ).astype(jnp.bfloat16)
    value_rows = projected[:, q_cols + k_cols :].astype(jnp.bfloat16)
    kv_all = lax.all_gather(
        jnp.concatenate([key_rows.reshape(tok_rows, -1), value_rows], axis=1),
        "ctx", axis=0, tiled=True,
    )
    all_keys = kv_all[:, :k_cols].reshape(-1, kv_here, HD)
    all_values = kv_all[:, k_cols:].reshape(-1, kv_here, HD)
    grouped = queries.reshape(tok_rows, kv_here, groups, HD)
    key_pos = jnp.arange(all_keys.shape[0])
    visible = (positions[:, None] >= key_pos[None, :])[None, None]

    def masked_scores():
        raw_scores = (
            jnp.einsum("qgjd,kgd->gjqk", grouped, all_keys, preferred_element_type=jnp.float32)
            * score_scale
        )
        return jnp.where(visible, raw_scores, masked_score)

    scores = masked_scores()
    row_max = jnp.max(scores, axis=-1, keepdims=True)
    exp_vals = jnp.exp(scores - row_max)
    exp_total = jnp.sum(exp_vals, axis=-1, keepdims=True)
    probability_low = (exp_vals / exp_total).astype(jnp.bfloat16)
    log_total = row_max + jnp.log(exp_total)
    attended = (
        jnp.einsum(
            "gjqk,kgd->qgjd", probability_low, all_values, preferred_element_type=jnp.float32
        )
        .reshape(tok_rows, -1)
        .astype(jnp.bfloat16)
    )
    partial_attn = jnp.einsum(
        "th,dh->td", attended, full_out, preferred_element_type=jnp.float32
    )
    hidden = tok_field + sum_tp(partial_attn)
    scale_two = rms_scale(hidden)
    normed_moe = (hidden * scale_two * gain_two).astype(jnp.bfloat16)

    moe_all = lax.all_gather(normed_moe, "shard", axis=0, tiled=True)

    def gates(logits, chosen):
        shown = jnp.where(chosen > 0, logits, masked_score)
        weights = jnp.where(
            chosen > 0, jnp.exp(shown - jnp.max(shown, axis=-1, keepdims=True)), 0.0
        )
        return weights / jnp.sum(weights, axis=-1, keepdims=True)

    gates_all = gates(
        jnp.dot(moe_all, full_router, preferred_element_type=jnp.float32),
        chosen_all.astype(jnp.float32),
    )
    gates_own = lax.dynamic_slice_in_dim(gates_all, shard_at * own, own, 1)
    gate_up = jnp.dot(moe_all, weight_gu, preferred_element_type=jnp.float32)
    back_down = jnp.dot(cot_all, weight_down, preferred_element_type=jnp.float32)
    gates_wide = jnp.repeat(gates_own, hidden_here, axis=1)
    gate_pre = gate_up[:, :span]
    up_pre = gate_up[:, span:]
    sigmoid_gate = jax.nn.sigmoid(gate_pre)
    activation = (gate_pre * sigmoid_gate * up_pre).astype(jnp.bfloat16).astype(jnp.float32)
    gated_act = (gates_wide * activation).astype(jnp.bfloat16)
    grad_gates_part = jnp.sum(
        (activation * back_down).reshape(-1, own, hidden_here), axis=-1
    )
    grad_activation = gates_wide * back_down
    grad_gu = jnp.concatenate(
        [
            (
                grad_activation * up_pre * sigmoid_gate * (1.0 + gate_pre * (1.0 - sigmoid_gate))
            ).astype(jnp.bfloat16),
            (grad_activation * gate_pre * sigmoid_gate).astype(jnp.bfloat16),
        ],
        axis=1,
    )
    partial_moe = jnp.einsum(
        "tf,df->td", gated_act, weight_down, preferred_element_type=jnp.float32
    ).astype(jnp.bfloat16)
    grad_moe_part = jnp.einsum(
        "tf,df->td", grad_gu, weight_gu, preferred_element_type=jnp.float32
    ).astype(jnp.bfloat16)
    out_rows = lax.psum_scatter(partial_moe, "shard", scatter_dimension=0, tiled=True)
    grad_moe_rows = lax.psum_scatter(grad_moe_part, "shard", scatter_dimension=0, tiled=True)
    placed_gates = lax.dynamic_update_slice_in_dim(
        jnp.zeros((expert_count, shards * tok_rows), jnp.float32),
        grad_gates_part.T, shard_at * own, 0,
    )
    grad_gates = lax.psum_scatter(placed_gates, "shard", scatter_dimension=1, tiled=True)
    grad_gates = (grad_gates + swap_tp(grad_gates)).T

    gating = gates(
        jnp.dot(normed_moe, full_router, preferred_element_type=jnp.float32), chosen_here
    )
    grad_logits = gating * (grad_gates - jnp.sum(gating * grad_gates, axis=-1, keepdims=True))
    grad_normed_moe = sum_tp(grad_moe_rows) + jnp.einsum(
        "te,de->td", grad_logits, full_router.astype(jnp.float32)
    )
    grad_router_full = jnp.einsum(
        "td,te->ed", normed_moe.astype(jnp.float32), grad_logits
    )
    grad_out = cotangent[0].astype(jnp.float32)
    grad_hidden_norm, grad_gain_two = norm_back(grad_normed_moe, hidden, scale_two, gain_two)
    grad_hidden = grad_out + grad_hidden_norm
    grad_branch = grad_hidden.astype(jnp.bfloat16)
    grad_attended_flat = jnp.dot(
        grad_branch, full_out, preferred_element_type=jnp.float32
    ).astype(jnp.bfloat16)

    expert_grads = jnp.concatenate(
        [
            jnp.einsum("td,tf->df", moe_all, grad_gu, preferred_element_type=jnp.float32),
            jnp.einsum("td,tf->df", cot_all, gated_act, preferred_element_type=jnp.float32),
        ],
        axis=1,
    ).astype(jnp.bfloat16)
    expert_grads = expert_grads.reshape(shards, ctxs, own_rows, 3 * span).transpose(1, 0, 2, 3)
    expert_grads = lax.optimization_barrier(
        expert_grads.reshape(ctxs * shards * own_rows, 3 * span)
    )
    expert_grads = lax.psum_scatter(expert_grads, "ctx", scatter_dimension=0, tiled=True)
    expert_grads = lax.all_to_all(
        expert_grads.reshape(shards, own_rows, 3 * span), "shard", split_axis=0, concat_axis=0, tiled=True
    ).reshape(shards, own_rows, 3, own, hidden_here)
    expert_grads = expert_grads.astype(jnp.float32)
    grad_gate_own = expert_grads[:, :, 0].transpose(0, 2, 1, 3).reshape(
        expert_count, own_rows, hidden_here)
    grad_up_own = expert_grads[:, :, 1].transpose(0, 2, 1, 3).reshape(
        expert_count, own_rows, hidden_here)
    grad_down_own = expert_grads[:, :, 2].transpose(0, 2, 3, 1).reshape(
        expert_count, hidden_here, own_rows)

    result = hidden + sum_tp(out_rows)
    output = result.astype(jnp.bfloat16)[None]

    grad_out_full = jnp.einsum(
        "td,th->dh", grad_branch, attended, preferred_element_type=jnp.float32
    ).astype(jnp.bfloat16)
    grad_out_own = scatter_sum(grad_out_full, own_rows).astype(jnp.float32).T
    small = lax.psum(
        jnp.concatenate([grad_router_full, grad_gain_two[None]], axis=0), ("shard", "ctx")
    )
    small = lax.dynamic_slice_in_dim(small, (shard_at * ctxs + ctx_at) * own_rows, own_rows, 1)
    grad_router_own = small[:expert_count].T
    grad_gain_m = small[expert_count]
    grad_attended = grad_attended_flat.reshape(tok_rows, kv_here, groups, HD)
    probability_again = jnp.exp(masked_scores() - log_total)
    grad_probability = jnp.einsum(
        "qgjd,kgd->gjqk", grad_attended, all_values, preferred_element_type=jnp.float32
    )
    grad_values_all = jnp.einsum(
        "gjqk,qgjd->kgd",
        probability_again.astype(jnp.bfloat16),
        grad_attended,
        preferred_element_type=jnp.float32,
    )
    inner_sum = jnp.sum(probability_again * grad_probability, axis=-1, keepdims=True)
    grad_scores = (probability_again * (grad_probability - inner_sum)).astype(jnp.bfloat16)
    grad_queries = (
        jnp.einsum("gjqk,kgd->qgjd", grad_scores, all_keys, preferred_element_type=jnp.float32)
        * score_scale
    )
    grad_keys_all = (
        jnp.einsum("gjqk,qgjd->kgd", grad_scores, grouped, preferred_element_type=jnp.float32)
        * score_scale
    )
    grad_kv_all = jnp.concatenate(
        [
            grad_keys_all.reshape(-1, k_cols).astype(jnp.bfloat16),
            grad_values_all.reshape(-1, k_cols).astype(jnp.bfloat16),
        ],
        axis=1,
    )
    grad_kv = lax.psum_scatter(grad_kv_all, "ctx", scatter_dimension=0, tiled=True).astype(
        jnp.float32
    )
    grad_query_rows = (
        rotate_back(grad_queries.reshape(tok_rows, heads_here, HD), positions)
        .reshape(tok_rows, -1)
        .astype(jnp.bfloat16)
    )
    grad_key_rows = (
        rotate_back(grad_kv[:, :k_cols].reshape(tok_rows, kv_here, HD), positions)
        .reshape(tok_rows, -1)
        .astype(jnp.bfloat16)
    )
    grad_value_rows = grad_kv[:, k_cols:].astype(jnp.bfloat16)
    grad_rows = jnp.concatenate([grad_query_rows, grad_key_rows, grad_value_rows], axis=1)
    grad_normed_part = jnp.einsum(
        "th,dh->td", grad_rows, full_qkv, preferred_element_type=jnp.float32
    )
    grad_normed = sum_tp(grad_normed_part)
    grad_qkv_full = jnp.einsum(
        "td,th->dh", normed, grad_rows, preferred_element_type=jnp.float32
    ).astype(jnp.bfloat16)
    grad_qkv_own = scatter_sum(grad_qkv_full, own_rows).astype(jnp.float32)
    grad_field_norm, _ = norm_back(grad_normed, tok_field, scale_one, gain_one)
    grad_gain_one = lax.psum(
        jnp.sum(grad_normed_part * tok_field * scale_one, axis=0), ("shard", "ctx", "tp")
    )
    grad_gain_a = lax.dynamic_slice_in_dim(
        grad_gain_one, (shard_at * ctxs + ctx_at) * own_rows, own_rows, 0
    )
    grad_tokens = (grad_hidden + grad_field_norm).astype(jnp.bfloat16)[None]
    return (
        output,
        grad_tokens,
        grad_gain_a,
        grad_gain_m,
        grad_qkv_own[:, :q_cols],
        grad_qkv_own[:, q_cols : q_cols + k_cols],
        grad_qkv_own[:, q_cols + k_cols :],
        grad_out_own,
        grad_router_own,
        grad_gate_own,
        grad_up_own,
        grad_down_own,
    )


def solution(mesh):
    placed = (
        P("shard", "ctx", None),
        P(),
        P(),
        P("shard", "tp"),
        P("shard", "tp"),
        P("shard", "tp"),
        P("tp", "shard"),
        P("shard", None),
        P(None, "shard", "tp"),
        P(None, "shard", "tp"),
        P(None, "tp", "shard"),
        P("shard", "ctx", None),
        P("shard", "ctx", None),
    )
    return jax.shard_map(
        per_device,
        mesh=mesh,
        in_specs=placed,
        out_specs=(
            P("shard", "ctx", None),
            P("shard", "ctx", None),
            P(("shard", "ctx")),
            P(("shard", "ctx")),
            P(("shard", "ctx"), "tp"),
            P(("shard", "ctx"), "tp"),
            P(("shard", "ctx"), "tp"),
            P("tp", ("shard", "ctx")),
            P(("shard", "ctx"), None),
            P(None, ("shard", "ctx"), "tp"),
            P(None, ("shard", "ctx"), "tp"),
            P(None, "tp", ("shard", "ctx")),
        ),
        check_vma=False,
    )
```

time: 1620 us -> 957 us (0.59)
  blocking collectives: 476 us -> 147 us
  matrix products: 331 us -> 184 us
  local copies, waits for them, and re-layouts: 158 us -> 45.1 us
  waiting for transfers between devices: 521 us -> 446 us
  other arithmetic: 74.8 us -> 97 us
    all_to_all x4 -> x0, blocking collectives: 298 us -> none  [the longest x1 120 us: per_device(): lax.all_to_all(grad_expert, 'shard', split_axis=0, concat_axis=1, tiled=T...]
    all_to_all x6 -> x2, waiting for transfers between devices: 143 us -> 0.01 us  [the longest x1 0.01 us: per_device(): lax.all_to_all(stacked, 'shard', split_axis=0, concat_axis=0, tiled=True)]
    dot_general x32 -> x15, matrix products: 239 us -> 97 us  [the longest x1 15 us: per_device(): jnp.dot(cot_all, weight_down, preferred_element_type=jnp.float32)]
    all_gather x4 -> x5, waiting for transfers between devices: 7.44 us -> 64.5 us  [the longest x1 40.8 us: per_device(): lax.all_gather(jnp.concatenate([key_rows.reshape(tok_rows, -1), value_row...]
    all_to_all x10 -> x1, local copies, waits for them, and re-layouts: 56.9 us -> 8.61 us  [per_device(): lax.all_to_all(stacked, 'shard', split_axis=0, concat_axis=0, tiled=True)]
    convert_element_type x5 -> x2, local copies, waits for them, and re-layouts: 51.6 us -> 4.68 us  [the longest x1 4.55 us: per_device(): expert_grads = expert_grads.astype(jnp.float32)]
    ppermute x0 -> x5, waiting for transfers between devices: none -> 42.9 us  [swap_tp(): return lax.ppermute(part, 'tp', [(0, 1), (1, 0)])]
    psum x3 -> x1, waiting for transfers between devices: 118 us -> 81.4 us  [per_device(): lax.psum(jnp.concatenate([grad_router_full, grad_gain_two[None]], axis=0)...]
  transfers between devices with their start and end apart: 23 -> 22, of which waited for: 13 -> 12; matrix products, arithmetic and copies ran while one was open for 16% -> 27% of each run, Pallas kernels for 0% -> 0%
where the time goes in v1:
time: 957 us; the launch traced here: 953 us
  waiting for transfers between devices  446 us (47%)
  matrix products  184 us (19%)
  blocking collectives  147 us (15%)
  other arithmetic  97 us (10%)
  local copies, waits for them, and re-layouts  45.1 us (5%)
  starting transfers between devices  18.6 us (2%)
  between operations  14.9 us (2%)
    reduce_scatter x1, waiting for transfers between devices, per_device(): lax.psum_scatter(expert_grads, 'ctx', scatter_dimension=0, tiled=True)  107 us
    all_gather x1, blocking collectives, per_device(): full_router = lax.all_gather(router_weight, 'shard', axis=0, tiled=True)  102 us
    psum x1, waiting for transfers between devices, per_device(): lax.psum(jnp.concatenate([grad_router_full, grad_gain_two[None]], axis=0)...  81.4 us
    reduce_scatter x1, waiting for transfers between devices, per_device(): lax.psum_scatter(partial_moe, 'shard', scatter_dimension=0, tiled=True)  45.6 us
    ppermute x5, waiting for transfers between devices, swap_tp(): return lax.ppermute(part, 'tp', [(0, 1), (1, 0)])  42.9 us
    all_gather x1, waiting for transfers between devices, per_device(): lax.all_gather(jnp.concatenate([key_rows.reshape(tok_rows, -1), value_row...  40.8 us
    psum x1, blocking collectives, per_device(): lax.psum(jnp.sum(grad_normed_part * tok_field * scale_one, axis=0), ('sha...  39.4 us
    reduce_scatter x1, waiting for transfers between devices, per_device(): lax.psum_scatter(grad_moe_part, 'shard', scatter_dimension=0, tiled=True)  34.1 us
  transfers between devices with their start and end apart: 22, of which 12 were waited for; matrix products, arithmetic and copies ran while one was open for 27% of the time, Pallas kernels for 0%

profile of v1, /device:TPU:0, one launch (start us, length us, event | category | flops | bytes accessed | tf_op | source)
XLA Modules:
  0.0 952.7 jit_solution(1664949227771641040)
XLA Ops:
  7.2 1.9 pad_maximum_fusion.11
  10.0 1.5 fusion.37
  11.8 23.6 %all-gather.7.cloned.1.call-done = bf16[1024,1024]{1,0:T(8,128)(2,1)} async-done(((bf16[256,1024]{1,0:T(8,128)(2,1)}), bf16[1024,1024]{1,0:T(8,128)(2,1)}) %all-gather.7.cloned.1.call-update) | async-done | bytes 2097168 | tf_op jit(solution)/shard_map/all_gather | solution.py:111
  35.5 3.2 fusion.53
  42.3 1.8 iota_compare_fusion
  46.6 40.8 %all-gather.9.cloned.1.call-done = bf16[2048,512]{1,0:T(8,128)(2,1)} async-done(((bf16[512,512]{1,0:T(8,128)(2,1)}), bf16[2048,512]{1,0:T(8,128)(2,1)}) %all-gather.9.cloned.1.call-update) | async-done | bytes 2097168 | tf_op jit(solution)/shard_map/all_gather | solution.py:152
  87.4 1.7 fusion.67
  90.4 15.1 %fusion.70 = (f32[4,2,512]{2,1,0:T(2,128)S(1)}, f32[4,2,512,2048]{2,3,1,0:T(8,128)}) fusion(bf16[2048,4,64,1]{0,2,3,1:T(8,128)(2,1)S(1)} %bitcast.206, bf16[512,4,2,32]{0,3,2,1:T(8,128)(2,1)} %bitcast.220, bf16[512,4,2,32]{0,3,2,1:T(8,128)(2,1)S(1)} %bitcast.218, pred[512,2048]{0,1:T(8,128)(4,1)} %iota_compare_fusion), kind=kOutput, calls=%fused_computation.145 | convolution fusion | flops 1099952128 | bytes 36192256 | tf_op jit(solution)/shard_map/qgjd,kgd->gjqk/dot_general | solution.py:164
  105.5 13.1 %fusion.3 = f32[4,2,512]{2,1,0:T(2,128)S(1)} fusion(f32[4,2,512,2048]{2,3,1,0:T(8,128)} %get-tuple-element.47, f32[4,2,512]{2,1,0:T(2,128)S(1)} %get-tuple-element.46), kind=kLoop, calls=%fused_computation.9 | loop fusion | flops 16773120 | bytes 33587200 | tf_op jit(solution)/shard_map/reduce_sum | solution.py:172
  118.6 13.6 %fusion.46 = bf16[4,64,2,512]{3,1,2,0:T(8,128)(2,1)S(1)} fusion(bf16[2048,4,64,1]{0,2,3,1:T(8,128)(2,1)S(1)} %bitcast.203, f32[4,2,512,2048]{2,3,1,0:T(8,128)} %get-tuple-element.47, f32[4,2,512]{2,1,0:T(2,128)S(1)} %fusion.3, f32[4,2,512]{2,1,0:T(2,128)S(1)} %get-tuple-element.46), kind=kOutput, calls=%fused_computation.79 | convolution fusion | flops 1099169792 | bytes 35160064 | tf_op jit(solution)/shard_map/gjqk,kgd->qgjd/dot_general | solution.py:176
  132.3 2.1 convolution_convert_fusion.3
  134.4 1.6 collective-permute-start
  136.0 23.4 %collective-permute-done = bf16[512,1024]{1,0:T(8,128)(2,1)S(1)} collective-permute-done((bf16[512,1024]{1,0:T(8,128)(2,1)S(1)}, bf16[512,1024]{1,0:T(8,128)(2,1)S(1)}, u32[]{:S(2)}, u32[]{:S(2)}) %collective-permute-start) | collective-permute-done | bytes 1048608 | tf_op jit(solution)/shard_map/ppermute | solution.py:62
  161.4 4.0 copy.80
  165.4 4.0 copy.81
  169.5 6.6 pad_maximum_fusion.1
  176.1 5.3 all-to-all-start
  182.1 102.4 %all_gather.26 = bf16[1024,16]{0,1:T(8,128)(2,1)S(1)} all-gather(bf16[256,16]{0,1:T(8,128)(2,1)S(1)} %copy-done.32), channel_id=1, replica_groups=mesh['shard'=4,'ctx'=4,'tp'=2] {'shard'}, dimensions={0}, use_global_device_ids=true | all-gather | bytes 40960 | tf_op jit(solution)/shard_map/all_gather | solution.py:116
  284.6 5.4 all_gather.24
  290.0 8.6 copy.82
  298.6 3.5 fusion.72
  302.3 14.2 %fusion.19 = f32[2048,2048]{0,1:T(8,128)} fusion(bf16[2048,1024]{1,0:T(8,128)(2,1)S(1)} %copy-done.4, bf16[1024,3072]{1,0:T(8,128)(2,1)} %bitcast.197), kind=kOutput, calls=%fused_computation.42 | convolution fusion | flops 8589934592 | bytes 25165824 | tf_op jit(solution)/shard_map/dot_general | solution.py:203
  316.5 15.0 %bitcast_reduce_fusion = (f32[2048,4]{0,1:T(4,128)S(1)}, bf16[2048,1024]{0,1:T(8,128)(2,1)}, f32[1024,2048]{1,0:T(8,128)}) fusion(f32[2048,2048]{0,1:T(8,128)} %fusion.19, bf16[1,2048,1024]{2,1,0:T(8,128)(2,1)} %all-gather.15.cloned.1.call-done, bf16[1024,3072]{1,0:T(8,128)(2,1)} %bitcast.198), kind=kOutput, calls=%fused_computation.19 | convolution fusion | flops 4313833472 | bytes 35684352 | tf_op jit(solution)/shard_map/dot_general | solution.py:204
  331.4 15.3 %multiply_convert_fusion.1 = (bf16[2048,1024]{0,1:T(8,128)(2,1)S(1)}, bf16[2048,1024]{0,1:T(8,128)(2,1)}, bf16[2048,1024]{0,1:T(8,128)(2,1)}) fusion(f32[1024,2048]{1,0:T(8,128)} %get-tuple-element.48, f32[2048,2048]{0,1:T(8,128)} %fusion.19, f32[2048,4]{0,1:T(4,128)S(1)} %dynamic-slice_divide_fusion, bf16[2048,1024]{0,1:T(8,128)(2,1)} %get-tuple-element.17), kind=kLoop, calls=%fused_computation.21 | loop fusion | flops 35651584 | bytes 41975808 | tf_op jit(solution)/shard_map/convert_element_type | solution.py:219
  346.7 2.0 copy-done.9
  348.7 13.7 %fusion.16 = bf16[2048,1024]{1,0:T(8,128)(2,1)} fusion(bf16[2048,1024]{0,1:T(8,128)(2,1)} %get-tuple-element.23, bf16[2048,1024]{0,1:T(8,128)(2,1)S(1)} %get-tuple-element.22, bf16[1024,3072]{1,0:T(8,128)(2,1)} %bitcast.199), kind=kOutput, calls=%fused_computation.38 | convolution fusion | flops 8608808960 | bytes 16777216 | tf_op jit(solution)/shard_map/tf,df->td/dot_general | solution.py:227
  363.3 9.5 convolution_convert_fusion
  373.0 34.1 %reduce-scatter.12.cloned.1.call-done = bf16[512,1024]{1,0:T(8,128)(2,1)} async-done(((bf16[2048,1024]{1,0:T(8,128)(2,1)}), bf16[512,1024]{1,0:T(8,128)(2,1)}) %reduce-scatter.12.cloned.1.call-update) | async-done | bytes 1048592 | tf_op jit(solution)/shard_map/reduce_scatter | solution.py:231
  407.1 1.5 collective-permute-start.2
  409.0 20.9 %reduce-scatter.14.cloned.1.call-done = f32[16,512]{1,0:T(8,128)} async-done(((f32[16,2048]{1,0:T(8,128)}), f32[16,512]{1,0:T(8,128)}) %reduce-scatter.14.cloned.1.call-update) | async-done | bytes 32784 | tf_op jit(solution)/shard_map/reduce_scatter | solution.py:236
  429.9 1.5 collective-permute-start.3
  431.3 45.6 %reduce-scatter.10.cloned.1.call-done = bf16[512,1024]{1,0:T(8,128)(2,1)} async-done(((bf16[2048,1024]{1,0:T(8,128)(2,1)}), bf16[512,1024]{1,0:T(8,128)(2,1)}) %reduce-scatter.10.cloned.1.call-update) | async-done | bytes 1048592 | tf_op jit(solution)/shard_map/reduce_scatter | solution.py:230
  476.9 1.5 collective-permute-start.1
  480.0 2.5 multiply_reduce_fusion
  482.5 19.5 %collective-permute-done.1 = bf16[512,1024]{1,0:T(8,128)(2,1)S(1)} collective-permute-done((bf16[512,1024]{1,0:T(8,128)(2,1)}, bf16[512,1024]{1,0:T(8,128)(2,1)S(1)}, u32[]{:S(2)}, u32[]{:S(2)}) %collective-permute-start.1) | collective-permute-done | bytes 1048608 | tf_op jit(solution)/shard_map/ppermute | solution.py:62
  502.0 4.2 convert_add_fusion.1
  506.2 1.7 convolution_convert_fusion.2
  508.0 2.1 convolution_convert_fusion.4
  510.1 22.3 %fusion = (f32[4,2,512]{2,1,0:T(2,128)S(1)}, f32[4,2048,512,2]{2,1,3,0:T(8,128)}) fusion(f32[4,2,512,2048]{2,3,1,0:T(8,128)} %get-tuple-element.47, f32[4,2,512]{2,1,0:T(2,128)S(1)} %bitcast.236, bf16[2048,4,64,1]{0,2,3,1:T(8,128)(2,1)S(1)} %bitcast.204, bf16[512,4,2,64]{0,3,2,1:T(8,128)(2,1)S(1)} %bitcast.201), kind=kOutput, calls=%fused_computation.2 | convolution fusion | flops 1098903552 | bytes 68714496 | tf_op jit(solution)/shard_map/qgjd,kgd->gjqk/dot_general | solution.py:295
  532.4 27.8 %fusion.2 = bf16[4,2,512,2048]{2,3,1,0:T(8,128)(2,1)} fusion(f32[4,2048,512,2]{2,1,3,0:T(8,128)} %get-tuple-element.55, f32[4,2,512,2048]{2,3,1,0:T(8,128)} %get-tuple-element.47, f32[4,2,512]{2,1,0:T(2,128)S(1)} %get-tuple-element.54, f32[4,2,512]{2,1,0:T(2,128)S(1)} %bitcast.237), kind=kLoop, calls=%fused_computation.4 | loop fusion | flops 33554432 | bytes 83918848 | tf_op jit(solution)/shard_map/convert_element_type | solution.py:305
  560.2 12.0 %fusion.25 = bf16[4,64,2048]{2,1,0:T(8,128)(2,1)} fusion(bf16[4,2,512,2048]{2,3,1,0:T(8,128)(2,1)} %fusion.2, bf16[512,4,2,32]{0,3,2,1:T(8,128)(2,1)} %bitcast.221, bf16[512,4,2,32]{0,3,2,1:T(8,128)(2,1)S(1)} %bitcast.219), kind=kOutput, calls=%fused_computation.47 | convolution fusion | flops 1075838976 | bytes 18350080 | tf_op jit(solution)/shard_map/gjqk,qgjd->kgd/dot_general | solution.py:311
  572.1 14.4 %fusion.26 = bf16[4,64,2048]{2,1,0:T(8,128)(2,1)} fusion(bf16[512,4,2,64]{0,3,2,1:T(8,128)(2,1)} %bitcast.202, f32[4,2,512,2048]{2,3,1,0:T(8,128)} %get-tuple-element.47, f32[4,2,512]{2,1,0:T(2,128)S(1)} %bitcast.238), kind=kOutput, calls=%fused_computation.48 | convolution fusion | flops 1091043328 | bytes 35143680 | tf_op jit(solution)/shard_map/gjqk,qgjd->kgd/dot_general | solution.py:298
  586.5 3.2 pad_maximum_fusion.9
  590.0 9.5 fusion.41
  599.5 11.0 %fusion.17 = bf16[1024,2048]{1,0:T(8,128)(2,1)} fusion(bf16[2048,1024]{1,0:T(8,128)(2,1)S(1)} %copy-done.5, bf16[2048,1024]{0,1:T(8,128)(2,1)} %get-tuple-element.23, bf16[2048,1024]{0,1:T(8,128)(2,1)S(1)} %copy-done.10), kind=kOutput, calls=%fused_computation.39 | convolution fusion | flops 8608808960 | bytes 16777216 | tf_op jit(solution)/shard_map/td,tf->df/dot_general | solution.py:259
  610.6 3.5 pad_maximum_fusion.2
  614.1 3.2 copy.99
  618.5 9.0 convolution_multiply_fusion
  628.6 1.8 pad_maximum_fusion.14
  630.4 3.5 reduce-scatter.16.cloned.1.call-done
  635.2 3.9 convolution_convert_fusion.1
  639.2 107.3 %reduce-scatter.26.cloned.1.call-done = bf16[256,3072]{1,0:T(8,128)(2,1)} async-done(((bf16[1024,3072]{1,0:T(8,128)(2,1)}), bf16[256,3072]{1,0:T(8,128)(2,1)}) %reduce-scatter.26.cloned.1.call-update) | async-done | bytes 1572880 | tf_op jit(solution)/shard_map/reduce_scatter | solution.py:268
  746.4 4.4 all-to-all-start.1
  750.9 4.8 fusion.73
  755.7 1.5 collective-permute-start.4
  757.1 81.4 %all-reduce.2.cloned.1.call-done = f32[17,1024]{1,0:T(8,128)} async-done(((f32[17,1024]{1,0:T(8,128)}), f32[17,1024]{1,0:T(8,128)}) %all-reduce.2.cloned.1.call-update) | async-done | bytes 69648 | tf_op jit(solution)/shard_map/psum | solution.py:287
  841.2 18.2 %reduce-scatter.24.cloned.1.call-done = bf16[1,64,512]{2,1,0:T(8,128)(2,1)} async-done(((bf16[4,64,512]{2,1,0:T(8,128)(2,1)}), bf16[1,64,512]{2,1,0:T(8,128)(2,1)}) %reduce-scatter.24.cloned.1.call-update) | async-done | bytes 65552 | tf_op jit(solution)/shard_map/reduce_scatter | solution.py:77
  859.4 1.5 convert_bitcast_fusion
  860.9 4.5 reshape.264
  865.4 26.2 %reduce-scatter.18.cloned.1.call-done = bf16[1,4,64,1024]{3,2,1,0:T(8,128)(2,1)} async-done(((bf16[4,4,64,1024]{3,2,1,0:T(8,128)(2,1)}), bf16[1,4,64,1024]{3,2,1,0:T(8,128)(2,1)}) %reduce-scatter.18.cloned.1.call-update) | async-done | bytes 524304 | tf_op jit(solution)/shard_map/reduce_scatter | solution.py:71
  891.7 2.6 slice_bitcast_fusion
  897.8 2.5 fusion.40
  900.2 39.4 %psum.14 = f32[1024]{0:T(1024)S(1)} all-reduce(f32[1024]{0:T(1024)S(1)} %get-tuple-element.14), channel_id=1, replica_groups=mesh['shard'=4,'ctx'=4,'tp'=2] {'shard','ctx','tp'}, use_global_device_ids=true, to_apply=%region_19.20 | all-reduce | flops 1024 | bytes 8192 | tf_op jit(solution)/shard_map/psum | solution.py:345
  940.2 3.4 fusion.48
  (157 shorter events, 27.1 us)
Async XLA Ops:
  7.2 28.3 %all-gather.7.cloned.1.call-start = ((), (), s32[]{:S(2)}) async-start(), calls=%async_computation.11 | async-start | bytes 2621440 | tf_op jit(solution)/shard_map/all_gather | solution.py:111
  9.2 78.2 %all-gather.9.cloned.1.call-start = ((), (), s32[]{:S(2)}) async-start(), calls=%async_computation.12 | async-start | bytes 2621440 | tf_op jit(solution)/shard_map/all_gather | solution.py:152
  9.9 28.8 %copy-start.27 = (f32[1024]{0:T(1024)}, f32[1024]{0:T(1024)S(1)}, u32[]{:S(2)}) copy-start(f32[1024]{0:T(1024)S(1)} %convert_element_type.185) | copy-start | bytes 12292
  11.5 27.3 %copy-start.29 = (f32[512]{0:T(512)}, f32[512]{0:T(512)S(1)}, u32[]{:S(2)}) copy-start(f32[512]{0:T(512)S(1)} %add_rsqrt_fusion.1) | copy-start | bytes 6148
  11.8 33.9 %copy-start.15 = (f32[512,32]{0,1:T(8,128)}, f32[512,32]{0,1:T(8,128)S(1)}, u32[]{:S(2)}) copy-start(f32[512,32]{0,1:T(8,128)S(1)} %get-tuple-element.44) | copy-start | bytes 196612
  11.8 33.9 %copy-start.17 = (f32[512,32]{0,1:T(8,128)}, f32[512,32]{0,1:T(8,128)S(1)}, u32[]{:S(2)}) copy-start(f32[512,32]{0,1:T(8,128)S(1)} %get-tuple-element.45) | copy-start | bytes 196612
  38.7 1.3 copy-start.19
  41.4 90.9 %all-gather.11.cloned.1.call-start = ((), (), s32[]{:S(2)}) async-start(), calls=%async_computation.13 | async-start | bytes 1310720 | tf_op jit(solution)/shard_map/all_gather | solution.py:115
  42.1 256.5 %all-gather.13.cloned.1.call-start = ((), (), s32[]{:S(2)}) async-start(), calls=%async_computation.14 | async-start | bytes 5242880 | tf_op jit(solution)/shard_map/all_gather | solution.py:189
  46.6 43.8 %copy-start.20 = (bf16[512,8,32]{0,2,1:T(8,128)(2,1)}, bf16[512,8,32]{0,2,1:T(8,128)(2,1)S(1)}, u32[]{:S(2)}) copy-start(bf16[512,8,32]{0,2,1:T(8,128)(2,1)S(1)} %get-tuple-element.33) | copy-start | bytes 786436
  89.8 15.8 %copy-start.11 = (bf16[2048,256]{0,1:T(8,128)(2,1)}, bf16[2048,256]{0,1:T(8,128)(2,1)S(1)}, u32[]{:S(2)}) copy-start(bf16[2048,256]{0,1:T(8,128)(2,1)S(1)} %copy.77) | copy-start | bytes 3145732
  90.4 28.2 %copy-start.7 = (bf16[2048,256]{0,1:T(8,128)(2,1)}, bf16[2048,256]{0,1:T(8,128)(2,1)S(1)}, u32[]{:S(2)}) copy-start(bf16[2048,256]{0,1:T(8,128)(2,1)S(1)} %copy.76) | copy-start | bytes 3145732
  118.6 17.4 %copy-start.33 = (bf16[1024]{0:T(1024)(128)(2,1)S(1)}, bf16[1024]{0:T(1024)(128)(2,1)}, u32[]{:S(2)}) copy-start(bf16[1024]{0:T(1024)(128)(2,1)} %param.15) | copy-start | bytes 6148
  118.6 40.8 %copy-start.2 = (bf16[1,512,1024]{2,1,0:T(8,128)(2,1)S(1)}, bf16[1,512,1024]{2,1,0:T(8,128)(2,1)}, u32[]{:S(2)}) copy-start(bf16[1,512,1024]{2,1,0:T(8,128)(2,1)} %param.13) | copy-start | bytes 3145732
  132.2 3.8 copy-start.23
  134.4 25.0 %collective-permute-start = (bf16[512,1024]{1,0:T(8,128)(2,1)S(1)}, bf16[512,1024]{1,0:T(8,128)(2,1)S(1)}, u32[]{:S(2)}, u32[]{:S(2)}) collective-permute-start(bf16[512,1024]{1,0:T(8,128)(2,1)S(1)} %convolution_convert_fusion.3), channel_id=1, source_target_pairs={{0,1},{1,0},{2,3},{3,2},{4,5},{5,4},{6,7},{7,6},{8,9},{9,8},{10,11... | collective-permute-start | bytes 3145736 | tf_op jit(solution)/shard_map/ppermute | solution.py:62
  160.0 320.0 %copy-start = (f32[512,1024]{1,0:T(8,128)}, f32[512,1024]{1,0:T(8,128)S(1)}, u32[]{:S(2)}) copy-start(f32[512,1024]{1,0:T(8,128)S(1)} %get-tuple-element.21) | copy-start | bytes 6291460
  176.1 6.0 copy-start.31
  176.1 6.1 copy-start.32
  176.1 113.9 %all-to-all-start = ((bf16[4,256,3072]{1,2,0:T(8,128)(2,1)}), bf16[4,256,3072]{1,2,0:T(8,128)(2,1)}, u32[]{:S(2)}, u32[]{:S(2)}) async-start(bf16[4,256,3072]{1,2,0:T(8,128)(2,1)} %bitcast.194), calls=%async_computation | async-start | bytes 12582912 | tf_op jit(solution)/shard_map/all_to_all | solution.py:121
  181.4 135.1 %all-gather.15.cloned.1.call-start = ((), (), s32[]{:S(2)}) async-start(), calls=%async_computation.25 | async-start | bytes 5242880 | tf_op jit(solution)/shard_map/all_gather | solution.py:133
  182.0 225.1 %reduce-scatter.12.cloned.1.call-start = ((), (), s32[]{:S(2)}) async-start(), calls=%async_computation.16 | async-start | bytes 5242880 | tf_op jit(solution)/shard_map/reduce_scatter | solution.py:231
  298.6 3.6 copy-start.4
  346.7 2.0 copy-start.9
  362.4 67.4 %reduce-scatter.14.cloned.1.call-start = ((), (), s32[]{:S(2)}) async-start(), calls=%async_computation.17 | async-start | bytes 163840 | tf_op jit(solution)/shard_map/reduce_scatter | solution.py:236
  362.5 0.7 copy-start.25
  363.2 113.7 %reduce-scatter.10.cloned.1.call-start = ((), (), s32[]{:S(2)}) async-start(), calls=%async_computation.15 | async-start | bytes 5242880 | tf_op jit(solution)/shard_map/reduce_scatter | solution.py:230
  372.7 35.8 %copy-start.1 = (bf16[512,1024]{1,0:T(8,128)(2,1)S(1)}, bf16[512,1024]{1,0:T(8,128)(2,1)}, u32[]{:S(2)}) copy-start(bf16[512,1024]{1,0:T(8,128)(2,1)} %multiply_convert_fusion.3) | copy-start | bytes 3145732
  372.8 257.6 %reduce-scatter.22.cloned.1.call-start = ((), (), s32[]{:S(2)}) async-start(), calls=%async_computation.22 | async-start | bytes 1310720 | tf_op jit(solution)/shard_map/reduce_scatter | solution.py:71
  407.1 72.9 %collective-permute-start.2 = (bf16[512,1024]{1,0:T(8,128)(2,1)}, bf16[512,1024]{1,0:T(8,128)(2,1)}, u32[]{:S(2)}, u32[]{:S(2)}) collective-permute-start(bf16[512,1024]{1,0:T(8,128)(2,1)} %reduce-scatter.12.cloned.1.call-done), channel_id=1, source_target_pairs={{0,1},{1,0},{2,3},{3,2},{4,5},{5,4},{6,7},{7,6},{8,9},{9,8},{10,11... | collective-permute-start | bytes 3145736 | tf_op jit(solution)/shard_map/ppermute | solution.py:62
  429.9 48.5 %collective-permute-start.3 = (f32[16,512]{1,0:T(8,128)}, f32[16,512]{1,0:T(8,128)S(1)}, u32[]{:S(2)}, u32[]{:S(2)}) collective-permute-start(f32[16,512]{1,0:T(8,128)} %reduce-scatter.14.cloned.1.call-done), channel_id=1, source_target_pairs={{0,1},{1,0},{2,3},{3,2},{4,5},{5,4},{6,7},{7,6},{8,9},{9,8},{10,11... | collective-permute-start | bytes 98312 | tf_op jit(solution)/shard_map/ppermute | solution.py:62
  476.9 25.1 %copy-start.12 = (bf16[1,512,1024]{2,1,0:T(8,128)(2,1)S(1)}, bf16[1,512,1024]{2,1,0:T(8,128)(2,1)}, u32[]{:S(2)}) copy-start(bf16[1,512,1024]{2,1,0:T(8,128)(2,1)} %param.25) | copy-start | bytes 3145732
  476.9 25.1 %copy-start.13 = (bf16[512,1024]{1,0:T(8,128)(2,1)S(1)}, bf16[512,1024]{1,0:T(8,128)(2,1)}, u32[]{:S(2)}) copy-start(bf16[512,1024]{1,0:T(8,128)(2,1)} %reduce-scatter.12.cloned.1.call-done) | copy-start | bytes 3145732
  476.9 25.1 %copy-start.22 = (bf16[512,1024]{1,0:T(8,128)(2,1)S(1)}, bf16[512,1024]{1,0:T(8,128)(2,1)}, u32[]{:S(2)}) copy-start(bf16[512,1024]{1,0:T(8,128)(2,1)} %reduce-scatter.10.cloned.1.call-done) | copy-start | bytes 3145732
  476.9 25.1 %collective-permute-start.1 = (bf16[512,1024]{1,0:T(8,128)(2,1)}, bf16[512,1024]{1,0:T(8,128)(2,1)S(1)}, u32[]{:S(2)}, u32[]{:S(2)}) collective-permute-start(bf16[512,1024]{1,0:T(8,128)(2,1)} %reduce-scatter.10.cloned.1.call-done), channel_id=1, source_target_pairs={{0,1},{1,0},{2,3},{3,2},{4,5},{5,4},{6,7},{7,6},{8,9},{9,8},{10,11... | collective-permute-start | bytes 3145736 | tf_op jit(solution)/shard_map/ppermute | solution.py:62
  502.0 4.2 copy-start.24
  508.0 125.9 %reduce-scatter.16.cloned.1.call-start = ((), (), s32[]{:S(2)}) async-start(), calls=%async_computation.18 | async-start | bytes 2621440 | tf_op jit(solution)/shard_map/reduce_scatter | solution.py:321
  508.0 2.1 copy-start.8
  510.1 22.3 %copy-start.6 = (bf16[512,512]{0,1:T(8,128)(2,1)}, bf16[512,512]{0,1:T(8,128)(2,1)S(1)}, u32[]{:S(2)}) copy-start(bf16[512,512]{0,1:T(8,128)(2,1)S(1)} %convolution_convert_fusion.4) | copy-start | bytes 1572868
  532.4 27.8 %copy-start.21 = (bf16[512,8,32]{0,2,1:T(8,128)(2,1)S(1)}, bf16[512,8,32]{0,2,1:T(8,128)(2,1)}, u32[]{:S(2)}) copy-start(bf16[512,8,32]{0,2,1:T(8,128)(2,1)} %copy-done.20) | copy-start | bytes 786436
  589.8 156.7 %reduce-scatter.26.cloned.1.call-start = ((), (), s32[]{:S(2)}) async-start(), calls=%async_computation.24 | async-start | bytes 7864320 | tf_op jit(solution)/shard_map/reduce_scatter | solution.py:268
  590.0 9.5 copy-start.5
  590.0 9.5 copy-start.10
  617.3 221.2 %all-reduce.2.cloned.1.call-start = ((), (), s32[]{:S(2)}) async-start(), calls=%async_computation.19 | async-start | bytes 196608 | tf_op jit(solution)/shard_map/psum | solution.py:287
  618.5 9.1 copy-start.16
  618.5 9.1 copy-start.18
  627.6 7.6 copy-start.3
  627.6 7.6 copy-start.28
  627.6 7.6 copy-start.30
  628.5 230.9 %reduce-scatter.24.cloned.1.call-start = ((), (), s32[]{:S(2)}) async-start(), calls=%async_computation.23 | async-start | bytes 327680 | tf_op jit(solution)/shard_map/reduce_scatter | solution.py:77
  630.4 261.3 %reduce-scatter.18.cloned.1.call-start = ((), (), s32[]{:S(2)}) async-start(), calls=%async_computation.20 | async-start | bytes 2621440 | tf_op jit(solution)/shard_map/reduce_scatter | solution.py:71
  635.0 4.1 copy-start.26
  746.4 114.4 %all-to-all-start.1 = ((bf16[4,64,3072]{2,1,0:T(8,128)(2,1)}), bf16[4,64,3072]{2,1,0:T(8,128)(2,1)}, u32[]{:S(2)}, u32[]{:S(2)}) async-start(bf16[4,64,3072]{2,1,0:T(8,128)(2,1)} %bitcast.217), calls=%async_computation.10 | async-start | bytes 3145728 | tf_op jit(solution)/shard_map/all_to_all | solution.py:269
  750.8 192.8 %reduce-scatter.20.cloned.1.call-start = ((), (), s32[]{:S(2)}) async-start(), calls=%async_computation.21 | async-start | bytes 655360 | tf_op jit(solution)/shard_map/reduce_scatter | solution.py:77
  755.7 142.1 %collective-permute-start.4 = (bf16[512,1024]{1,0:T(8,128)(2,1)}, bf16[512,1024]{1,0:T(8,128)(2,1)}, u32[]{:S(2)}, u32[]{:S(2)}) collective-permute-start(bf16[512,1024]{1,0:T(8,128)(2,1)} %get-tuple-element.56), channel_id=1, source_target_pairs={{0,1},{1,0},{2,3},{3,2},{4,5},{5,4},{6,7},{7,6},{8,9},{9,8},{10,11... | collective-permute-start | bytes 3145736 | tf_op jit(solution)/shard_map/ppermute | solution.py:62
  894.3 3.5 copy-start.14
Sparse Core Ops, SparseCore 0:
  10.1 25.2 all-gather.6
  41.5 45.9 all-gather.8
  89.0 15.5 all-gather.10
  161.6 42.6 all-gather.12
  205.7 59.1 all-gather.14
  362.6 44.4 reduce-scatter.11
  410.2 19.5 reduce-scatter.13
  432.4 44.4 reduce-scatter.9
  508.1 24.8 reduce-scatter.21
  589.9 44.0 reduce-scatter.15
  636.3 110.0 reduce-scatter.25
  750.7 87.7 all-reduce.1
  840.8 18.5 reduce-scatter.23
  861.9 29.7 reduce-scatter.17
  893.8 21.6 reduce-scatter.19

commit v2 on v1

--- a/solution.py
+++ b/solution.py
@@ -65,6 +65,22 @@
 def sum_tp(part):
     low = part.astype(jnp.bfloat16)
     return low.astype(jnp.float32) + swap_tp(low).astype(jnp.float32)
+
+
+def widen(cols):
+    return jnp.pad(cols, ((0, 0), (0, 128 - cols.shape[1])))
+
+
+def exchange(blocks):
+    count = lax.axis_size("shard")
+    at = lax.axis_index("shard")
+    own_block = lax.dynamic_slice_in_dim(blocks, at, 1, 0)
+    arrived = lax.dynamic_update_slice_in_dim(jnp.zeros_like(blocks), own_block, at, 0)
+    for shift in range(1, count):
+        sent = lax.dynamic_slice_in_dim(blocks, (at + shift) % count, 1, 0)
+        got = lax.ppermute(sent, "shard", [(i, (i + shift) % count) for i in range(count)])
+        arrived = lax.dynamic_update_slice_in_dim(arrived, got, (at - shift) % count, 0)
+    return arrived
 
 
 def scatter_sum(grad, rows):
@@ -112,15 +128,18 @@
         jnp.concatenate([query_weight, key_weight, value_weight], axis=1),
         "shard", axis=0, tiled=True,
     )
-    full_out = lax.all_gather(out_weight.T, "shard", axis=0, tiled=True)
-    full_router = lax.all_gather(router_weight, "shard", axis=0, tiled=True)
+    head_cols = out_weight.shape[0]
+    out_router = lax.all_gather(
+        jnp.concatenate([out_weight.T, widen(router_weight)], axis=1),
+        "shard", axis=0, tiled=True,
+    )
+    full_out = out_router[:, :head_cols]
+    full_router = out_router[:, head_cols : head_cols + expert_count]
 
     stacked = jnp.stack([gate_weight, up_weight, jnp.swapaxes(down_weight, 1, 2)], axis=0)
     stacked = stacked.reshape(3, shards, own, width_here, hidden_here).transpose(1, 3, 0, 2, 4)
     stacked = stacked.reshape(shards, width_here, 3 * span)
-    expert_weights = lax.all_to_all(
-        stacked, "shard", split_axis=0, concat_axis=0, tiled=True
-    ).reshape(width, 3 * span)
+    expert_weights = exchange(stacked).reshape(width, 3 * span)
     weight_gu = expert_weights[:, : 2 * span]
     weight_down = expert_weights[:, 2 * span :]
     chosen_here = jnp.sum(
@@ -129,8 +148,12 @@
         ),
         axis=1,
     )
-    chosen_all = lax.all_gather(chosen_here.astype(jnp.bfloat16), "shard", axis=0, tiled=True)
-    cot_all = lax.all_gather(cotangent[0], "shard", axis=0, tiled=True)
+    cot_chosen = lax.all_gather(
+        jnp.concatenate([cotangent[0], widen(chosen_here.astype(jnp.bfloat16))], axis=1),
+        "shard", axis=0, tiled=True,
+    )
+    cot_all = cot_chosen[:, :width]
+    chosen_all = cot_chosen[:, width : width + expert_count]
 
     heads_here = q_cols // HD
     kv_here = k_cols // HD
@@ -227,24 +250,37 @@
     grad_moe_part = jnp.einsum(
         "tf,df->td", grad_gu, weight_gu, preferred_element_type=jnp.float32
     ).astype(jnp.bfloat16)
-    out_rows = lax.psum_scatter(partial_moe, "shard", scatter_dimension=0, tiled=True)
-    grad_moe_rows = lax.psum_scatter(grad_moe_part, "shard", scatter_dimension=0, tiled=True)
     placed_gates = lax.dynamic_update_slice_in_dim(
-        jnp.zeros((expert_count, shards * tok_rows), jnp.float32),
-        grad_gates_part.T, shard_at * own, 0,
-    )
-    grad_gates = lax.psum_scatter(placed_gates, "shard", scatter_dimension=1, tiled=True)
-    grad_gates = (grad_gates + swap_tp(grad_gates)).T
+        jnp.zeros((shards * tok_rows, 128), jnp.bfloat16),
+        grad_gates_part.astype(jnp.bfloat16), shard_at * own, 1,
+    )
+    back_rows = lax.psum_scatter(
+        jnp.concatenate([grad_moe_part, placed_gates], axis=1),
+        "shard", scatter_dimension=0, tiled=True,
+    )
+    expert_grads = jnp.concatenate(
+        [
+            jnp.einsum("td,tf->df", moe_all, grad_gu, preferred_element_type=jnp.float32),
+            jnp.einsum("td,tf->df", cot_all, gated_act, preferred_element_type=jnp.float32),
+        ],
+        axis=1,
+    ).astype(jnp.bfloat16)
+    expert_grads = expert_grads.reshape(shards, ctxs, own_rows, 3 * span).transpose(1, 0, 2, 3)
+    back_rows, expert_grads = lax.optimization_barrier(
+        (back_rows, expert_grads.reshape(ctxs * shards * own_rows, 3 * span))
+    )
+    back_sum = sum_tp(back_rows)
+    grad_gates = back_sum[:, width : width + expert_count]
 
     gating = gates(
         jnp.dot(normed_moe, full_router, preferred_element_type=jnp.float32), chosen_here
     )
     grad_logits = gating * (grad_gates - jnp.sum(gating * grad_gates, axis=-1, keepdims=True))
-    grad_normed_moe = sum_tp(grad_moe_rows) + jnp.einsum(
+    grad_normed_moe = back_sum[:, :width] + jnp.einsum(
         "te,de->td", grad_logits, full_router.astype(jnp.float32)
     )
     grad_router_full = jnp.einsum(
-        "td,te->ed", normed_moe.astype(jnp.float32), grad_logits
+        "td,te->de", normed_moe.astype(jnp.float32), grad_logits
     )
     grad_out = cotangent[0].astype(jnp.float32)
     grad_hidden_norm, grad_gain_two = norm_back(grad_normed_moe, hidden, scale_two, gain_two)
@@ -254,21 +290,10 @@
         grad_branch, full_out, preferred_element_type=jnp.float32
     ).astype(jnp.bfloat16)
 
-    expert_grads = jnp.concatenate(
-        [
-            jnp.einsum("td,tf->df", moe_all, grad_gu, preferred_element_type=jnp.float32),
-            jnp.einsum("td,tf->df", cot_all, gated_act, preferred_element_type=jnp.float32),
-        ],
-        axis=1,
-    ).astype(jnp.bfloat16)
-    expert_grads = expert_grads.reshape(shards, ctxs, own_rows, 3 * span).transpose(1, 0, 2, 3)
-    expert_grads = lax.optimization_barrier(
-        expert_grads.reshape(ctxs * shards * own_rows, 3 * span)
-    )
+    grad_attended_flat, partial_moe = lax.optimization_barrier((grad_attended_flat, partial_moe))
+    out_rows = lax.psum_scatter(partial_moe, "shard", scatter_dimension=0, tiled=True)
     expert_grads = lax.psum_scatter(expert_grads, "ctx", scatter_dimension=0, tiled=True)
-    expert_grads = lax.all_to_all(
-        expert_grads.reshape(shards, own_rows, 3 * span), "shard", split_axis=0, concat_axis=0, tiled=True
-    ).reshape(shards, own_rows, 3, own, hidden_here)
+    expert_grads = exchange(expert_grads.reshape(shards, own_rows, 3 * span)).reshape(shards, own_rows, 3, own, hidden_here)
     expert_grads = expert_grads.astype(jnp.float32)
     grad_gate_own = expert_grads[:, :, 0].transpose(0, 2, 1, 3).reshape(
         expert_count, own_rows, hidden_here)
@@ -283,13 +308,13 @@
     grad_out_full = jnp.einsum(
         "td,th->dh", grad_branch, attended, preferred_element_type=jnp.float32
     ).astype(jnp.bfloat16)
-    grad_out_own = scatter_sum(grad_out_full, own_rows).astype(jnp.float32).T
-    small = lax.psum(
-        jnp.concatenate([grad_router_full, grad_gain_two[None]], axis=0), ("shard", "ctx")
-    )
-    small = lax.dynamic_slice_in_dim(small, (shard_at * ctxs + ctx_at) * own_rows, own_rows, 1)
-    grad_router_own = small[:expert_count].T
-    grad_gain_m = small[expert_count]
+    extra = jnp.concatenate([grad_router_full, grad_gain_two[:, None]], axis=1)
+    grad_out_own = scatter_sum(
+        jnp.concatenate([grad_out_full, widen(extra.astype(jnp.bfloat16))], axis=1), own_rows
+    ).astype(jnp.float32)
+    grad_router_own = grad_out_own[:, head_cols : head_cols + expert_count]
+    grad_gain_m = grad_out_own[:, head_cols + expert_count]
+    grad_out_own = grad_out_own[:, :head_cols].T
     grad_attended = grad_attended_flat.reshape(tok_rows, kv_here, groups, HD)
     probability_again = jnp.exp(masked_scores() - log_total)
     grad_probability = jnp.einsum(
@@ -340,14 +365,14 @@
     grad_qkv_full = jnp.einsum(
         "td,th->dh", normed, grad_rows, preferred_element_type=jnp.float32
     ).astype(jnp.bfloat16)
-    grad_qkv_own = scatter_sum(grad_qkv_full, own_rows).astype(jnp.float32)
+    gain_one_part = jnp.sum(grad_normed_part * tok_field * scale_one, axis=0)[:, None]
+    grad_qkv_own = scatter_sum(
+        jnp.concatenate([grad_qkv_full, widen(gain_one_part.astype(jnp.bfloat16))], axis=1),
+        own_rows,
+    )
+    grad_gain_a = sum_tp(grad_qkv_own[:, q_cols + 2 * k_cols :])[:, 0]
+    grad_qkv_own = grad_qkv_own[:, : q_cols + 2 * k_cols].astype(jnp.float32)
     grad_field_norm, _ = norm_back(grad_normed, tok_field, scale_one, gain_one)
-    grad_gain_one = lax.psum(
-        jnp.sum(grad_normed_part * tok_field * scale_one, axis=0), ("shard", "ctx", "tp")
-    )
-    grad_gain_a = lax.dynamic_slice_in_dim(
-        grad_gain_one, (shard_at * ctxs + ctx_at) * own_rows, own_rows, 0
-    )
     grad_tokens = (grad_hidden + grad_field_norm).astype(jnp.bfloat16)[None]
     return (
         output,

time: 957 us -> 859 us (0.90)
  blocking collectives: 147 us -> 0 us
  local copies, waits for them, and re-layouts: 45.1 us -> 78.1 us
  waiting for transfers between devices: 446 us -> 463 us
    all_gather x2 -> x0, blocking collectives: 108 us -> none  [the longest x1 102 us: per_device(): full_router = lax.all_gather(router_weight, 'shard', axis=0, tiled=True)]
    psum x1 -> x0, waiting for transfers between devices: 81.4 us -> none  [per_device(): lax.psum(jnp.concatenate([grad_router_full, grad_gain_two[None]], axis=0)...]
    ppermute x0 -> x6, waiting for transfers between devices: none -> 75.2 us  [exchange(): lax.ppermute(sent, 'shard', [(i, (i + shift) % count) for i in range(coun...]
    psum x1 -> x0, blocking collectives: 39.4 us -> none  [per_device(): lax.psum(jnp.sum(grad_normed_part * tok_field * scale_one, axis=0), ('sha...]
    reduce_scatter x2 -> x1, waiting for transfers between devices: 55 us -> 23 us  [per_device(): lax.psum_scatter(jnp.concatenate([grad_moe_part, placed_gates], axis=1),...]
    reduce_scatter x2, waiting for transfers between devices: 26.2 us -> 53 us  [scatter_sum(): lax.psum_scatter(grad.reshape(lax.axis_size('shard'), lax.axis_size('ctx'...]
    reduce_scatter x2, waiting for transfers between devices: 18.2 us -> 42.8 us  [scatter_sum(): return lax.psum_scatter(parts, 'ctx', scatter_dimension=0, tiled=False)]
    reduce_scatter x1, waiting for transfers between devices: 3.5 us -> 27.8 us  [per_device(): lax.psum_scatter(grad_kv_all, 'ctx', scatter_dimension=0, tiled=True)]
  transfers between devices with their start and end apart: 22 -> 24, of which waited for: 12 -> 16; matrix products, arithmetic and copies ran while one was open for 27% -> 22% of each run, Pallas kernels for 0% -> 0%
where the time goes in v2:
time: 859 us; the launch traced here: 855 us
  waiting for transfers between devices  463 us (54%)
  matrix products  188 us (22%)
  other arithmetic  97 us (11%)
  local copies, waits for them, and re-layouts  78.1 us (9%)
  between operations  15 us (2%)
  starting transfers between devices  13.1 us (2%)
    reduce_scatter x1, waiting for transfers between devices, per_device(): lax.psum_scatter(expert_grads, 'ctx', scatter_dimension=0, tiled=True)  106 us
    ppermute x6, waiting for transfers between devices, exchange(): lax.ppermute(sent, 'shard', [(i, (i + shift) % count) for i in range(coun...  75.2 us
    reduce_scatter x2, waiting for transfers between devices, scatter_sum(): lax.psum_scatter(grad.reshape(lax.axis_size('shard'), lax.axis_size('ctx'...  53 us
    reduce_scatter x2, waiting for transfers between devices, scatter_sum(): return lax.psum_scatter(parts, 'ctx', scatter_dimension=0, tiled=False)  42.8 us
    ppermute x5, waiting for transfers between devices, swap_tp(): return lax.ppermute(part, 'tp', [(0, 1), (1, 0)])  38.3 us
    all_gather x1, waiting for transfers between devices, per_device(): lax.all_gather(jnp.concatenate([key_rows.reshape(tok_rows, -1), value_row...  37.6 us
    reduce_scatter x1, waiting for transfers between devices, per_device(): lax.psum_scatter(partial_moe, 'shard', scatter_dimension=0, tiled=True)  35.1 us
    reduce_scatter x1, waiting for transfers between devices, per_device(): lax.psum_scatter(grad_kv_all, 'ctx', scatter_dimension=0, tiled=True)  27.8 us
  transfers between devices with their start and end apart: 24, of which 16 were waited for; matrix products, arithmetic and copies ran while one was open for 22% of the time, Pallas kernels for 0%

profile of v2, /device:TPU:0, one launch (start us, length us, event | category | flops | bytes accessed | tf_op | source)
XLA Modules:
  0.0 854.9 jit_solution(11091164114048263583)
XLA Ops:
  7.2 2.0 pad_maximum_fusion.13
  12.5 23.0 %all-gather.6.cloned.1.call-done = bf16[1024,1024]{1,0:T(8,128)(2,1)} async-done(((bf16[256,1024]{1,0:T(8,128)(2,1)}), bf16[1024,1024]{1,0:T(8,128)(2,1)}) %all-gather.6.cloned.1.call-update) | async-done | bytes 2097168 | tf_op jit(solution)/shard_map/all_gather | solution.py:127
  35.5 2.9 fusion.63
  45.3 1.8 iota_compare_fusion.1
  49.6 37.6 %all-gather.8.cloned.1.call-done = bf16[2048,512]{1,0:T(8,128)(2,1)} async-done(((bf16[512,512]{1,0:T(8,128)(2,1)}), bf16[2048,512]{1,0:T(8,128)(2,1)}) %all-gather.8.cloned.1.call-update) | async-done | bytes 2097168 | tf_op jit(solution)/shard_map/all_gather | solution.py:175
  87.2 2.6 fusion.84
  90.5 1.9 copy.165
  92.4 15.2 %fusion.87 = (f32[4,2,512]{2,1,0:T(2,128)S(1)}, f32[4,2,512,2048]{2,3,1,0:T(8,128)}) fusion(bf16[2048,4,64,1]{0,2,3,1:T(8,128)(2,1)S(1)} %bitcast.160, bf16[512,4,2,32]{0,3,2,1:T(8,128)(2,1)} %bitcast.173, bf16[512,4,2,32]{0,3,2,1:T(8,128)(2,1)S(1)} %bitcast.171, pred[512,2048]{0,1:T(8,128)(4,1)} %iota_compare_fusion.1), kind=kOutput, calls=%fused_computation.180 | convolution fusion | flops 1099952128 | bytes 36192256 | tf_op jit(solution)/shard_map/qgjd,kgd->gjqk/dot_general | solution.py:187
  107.6 14.0 %fusion.3 = f32[4,2,512]{2,1,0:T(2,128)S(1)} fusion(f32[4,2,512,2048]{2,3,1,0:T(8,128)} %get-tuple-element.134, f32[4,2,512]{2,1,0:T(2,128)S(1)} %get-tuple-element.133), kind=kLoop, calls=%fused_computation.9 | loop fusion | flops 16773120 | bytes 33587200 | tf_op jit(solution)/shard_map/reduce_sum | solution.py:195
  121.6 13.7 %fusion.49 = bf16[4,64,2,512]{3,1,2,0:T(8,128)(2,1)S(1)} fusion(bf16[2048,4,64,1]{0,2,3,1:T(8,128)(2,1)S(1)} %bitcast.157, f32[4,2,512,2048]{2,3,1,0:T(8,128)} %get-tuple-element.134, f32[4,2,512]{2,1,0:T(2,128)S(1)} %fusion.3, f32[4,2,512]{2,1,0:T(2,128)S(1)} %get-tuple-element.133), kind=kOutput, calls=%fused_computation.87 | convolution fusion | flops 1099169792 | bytes 35160064 | tf_op jit(solution)/shard_map/gjqk,kgd->qgjd/dot_general | solution.py:199
  135.4 2.1 convolution_convert_fusion.3
  138.8 23.4 %collective-permute-done = bf16[512,1024]{1,0:T(8,128)(2,1)S(1)} collective-permute-done((bf16[512,1024]{1,0:T(8,128)(2,1)S(1)}, bf16[512,1024]{1,0:T(8,128)(2,1)S(1)}, u32[]{:S(2)}, u32[]{:S(2)}) %collective-permute-start) | collective-permute-done | bytes 1048608 | tf_op jit(solution)/shard_map/ppermute | solution.py:62
  164.1 3.9 copy.172
  168.0 4.0 copy.173
  172.0 3.9 pad_maximum_fusion.1
  175.9 2.8 constant_dynamic-slice_fusion.3
  181.9 2.6 copy.174
  184.5 3.5 broadcast_in_dim.45
  189.3 40.6 %collective-permute-done.1 = bf16[1,256,3072]{1,2,0:T(8,128)(2,1)} collective-permute-done((bf16[1,256,3072]{1,2,0:T(8,128)(2,1)}, bf16[1,256,3072]{1,2,0:T(8,128)(2,1)}, u32[]{:S(2)}, u32[]{:S(2)}) %collective-permute-start.1) | collective-permute-done | bytes 1572896 | tf_op jit(solution)/shard_map/ppermute | solution.py:81
  230.0 2.6 copy.175
  232.6 2.6 copy.176
  235.2 26.5 %collective-permute-done.3 = bf16[1,256,3072]{1,2,0:T(8,128)(2,1)} collective-permute-done((bf16[1,256,3072]{1,2,0:T(8,128)(2,1)}, bf16[1,256,3072]{1,2,0:T(8,128)(2,1)}, u32[]{:S(2)}, u32[]{:S(2)}) %collective-permute-start.3) | collective-permute-done | bytes 1572896 | tf_op jit(solution)/shard_map/ppermute | solution.py:81
  261.7 2.6 copy.177
  264.3 2.8 constant_dynamic-update-slice_fusion.5
  270.3 3.6 fusion.88
  273.9 1.7 fusion.83
  276.6 15.2 %fusion.16 = f32[2048,2048]{0,1:T(8,128)} fusion(bf16[2048,1024]{1,0:T(8,128)(2,1)} %all-gather.14.cloned.1.call-done, bf16[1024,3072]{1,0:T(8,128)(2,1)} %bitcast.27), kind=kOutput, calls=%fused_computation.41 | convolution fusion | flops 8589934592 | bytes 25165824 | tf_op jit(solution)/shard_map/dot_general | solution.py:226
  291.8 19.8 %multiply_convert_fusion.2 = (bf16[2048,1024]{0,1:T(8,128)(2,1)}, bf16[2048,1024]{0,1:T(8,128)(2,1)}, bf16[2048,1024]{0,1:T(8,128)(2,1)}, bf16[2048,1024]{0,1:T(8,128)(2,1)}, f32[2048,1024]{0,1:T(8,128)}) fusion(f32[2048,2048]{0,1:T(8,128)} %fusion.16, f32[2048,4]{0,1:T(4,128)S(1)} %copy.171, bf16[1024,3072]{1,0:T(8,128)(2,1)} %bitcast.27, ...), kind=kOutput, calls=%fused_computation.22 | convolution fusion | flops 4336910336 | bytes 48267264 | tf_op jit(solution)/shard_map/dot_general | solution.py:227
  311.5 5.9 bitcast_reduce_fusion
  317.8 13.9 %fusion.13 = bf16[2048,1024]{1,0:T(8,128)(2,1)} fusion(bf16[2048,1024]{0,1:T(8,128)(2,1)} %get-tuple-element.103, bf16[2048,1024]{0,1:T(8,128)(2,1)} %get-tuple-element.102, bf16[1024,3072]{1,0:T(8,128)(2,1)} %bitcast.27), kind=kOutput, calls=%fused_computation.37 | convolution fusion | flops 8608808960 | bytes 16777216 | tf_op jit(solution)/shard_map/tf,df->td/dot_general | solution.py:250
  331.8 2.4 dynamic_update_slice.31
  334.2 4.8 pad_maximum_fusion.5
  340.0 9.5 %fusion.44 = bf16[1024,1024]{1,0:T(8,128)(2,1)} fusion(bf16[2048,1024]{0,1:T(8,128)(2,1)} %get-tuple-element.104, bf16[2048,1152]{1,0:T(8,128)(2,1)} %all-gather.12.cloned.1.call-done), kind=kOutput, calls=%fused_computation.78 | convolution fusion | flops 4296015872 | bytes 10485760 | tf_op jit(solution)/shard_map/td,tf->df/dot_general | solution.py:264
  349.5 12.9 %fusion.14 = bf16[1024,2048]{1,0:T(8,128)(2,1)} fusion(bf16[2048,1024]{1,0:T(8,128)(2,1)} %all-gather.14.cloned.1.call-done, bf16[2048,1024]{0,1:T(8,128)(2,1)S(1)} %copy-done.10, bf16[2048,1024]{0,1:T(8,128)(2,1)S(1)} %copy-done.9), kind=kOutput, calls=%fused_computation.38 | convolution fusion | flops 8608808960 | bytes 16777216 | tf_op jit(solution)/shard_map/td,tf->df/dot_general | solution.py:263
  362.4 4.2 pad_maximum_fusion.2
  366.6 3.2 copy.205
  369.8 23.0 %reduce-scatter.9.cloned.1.call-done = bf16[512,1152]{1,0:T(8,128)(2,1)} async-done(((bf16[2048,1152]{1,0:T(8,128)(2,1)}), bf16[512,1152]{1,0:T(8,128)(2,1)}) %reduce-scatter.9.cloned.1.call-update) | async-done | bytes 1179664 | tf_op jit(solution)/shard_map/reduce_scatter | solution.py:257
  396.5 9.5 %convolution_convert_fusion = bf16[2048,1024]{1,0:T(8,128)(2,1)} fusion(bf16[2048,1024]{0,1:T(8,128)(2,1)} %get-tuple-element.104, bf16[1024,3072]{1,0:T(8,128)(2,1)} %bitcast.27), kind=kOutput, calls=%fused_computation.39 | convolution fusion | flops 4297064448 | bytes 10485760 | tf_op jit(solution)/shard_map/tf,df->td/dot_general | solution.py:247
  405.9 14.9 %collective-permute-done.4 = bf16[512,1152]{1,0:T(8,128)(2,1)} collective-permute-done((bf16[512,1152]{1,0:T(8,128)(2,1)}, bf16[512,1152]{1,0:T(8,128)(2,1)}, u32[]{:S(2)}, u32[]{:S(2)}) %collective-permute-start.4) | collective-permute-done | bytes 1179680 | tf_op jit(solution)/shard_map/ppermute | solution.py:62
  420.8 1.9 convert_add_fusion.1
  428.3 2.0 copy.184
  430.4 22.1 %fusion = (f32[4,2,512]{2,1,0:T(2,128)S(1)}, f32[4,2048,512,2]{2,1,3,0:T(8,128)}) fusion(f32[4,2,512,2048]{2,3,1,0:T(8,128)} %get-tuple-element.134, f32[4,2,512]{2,1,0:T(2,128)S(1)} %bitcast.189, bf16[2048,4,64,1]{0,2,3,1:T(8,128)(2,1)} %bitcast.158, bf16[512,4,2,64]{0,3,2,1:T(8,128)(2,1)} %bitcast.155), kind=kOutput, calls=%fused_computation.2 | convolution fusion | flops 1098903552 | bytes 68714496 | tf_op jit(solution)/shard_map/qgjd,kgd->gjqk/dot_general | solution.py:320
  452.5 14.6 %fusion.27 = bf16[4,64,2048]{2,1,0:T(8,128)(2,1)} fusion(bf16[512,4,2,64]{0,3,2,1:T(8,128)(2,1)} %bitcast.156, f32[4,2,512,2048]{2,3,1,0:T(8,128)} %get-tuple-element.134, f32[4,2,512]{2,1,0:T(2,128)S(1)} %bitcast.190), kind=kOutput, calls=%fused_computation.51 | convolution fusion | flops 1091043328 | bytes 35143680 | tf_op jit(solution)/shard_map/gjqk,qgjd->kgd/dot_general | solution.py:323
  467.1 27.7 %fusion.2 = bf16[4,2,512,2048]{2,3,1,0:T(8,128)(2,1)} fusion(f32[4,2048,512,2]{2,1,3,0:T(8,128)} %get-tuple-element.142, f32[4,2,512,2048]{2,3,1,0:T(8,128)} %get-tuple-element.134, f32[4,2,512]{2,1,0:T(2,128)S(1)} %get-tuple-element.141, f32[4,2,512]{2,1,0:T(2,128)S(1)} %bitcast.191), kind=kLoop, calls=%fused_computation.4 | loop fusion | flops 33554432 | bytes 83918848 | tf_op jit(solution)/shard_map/convert_element_type | solution.py:330
  494.9 12.0 %fusion.26 = bf16[4,64,2048]{2,1,0:T(8,128)(2,1)} fusion(bf16[4,2,512,2048]{2,3,1,0:T(8,128)(2,1)} %fusion.2, bf16[512,4,2,32]{0,3,2,1:T(8,128)(2,1)} %bitcast.174, bf16[512,4,2,32]{0,3,2,1:T(8,128)(2,1)S(1)} %bitcast.172), kind=kOutput, calls=%fused_computation.50 | convolution fusion | flops 1075838976 | bytes 18350080 | tf_op jit(solution)/shard_map/gjqk,qgjd->kgd/dot_general | solution.py:336
  506.8 3.2 pad_maximum_fusion.10
  511.8 1.8 convolution_convert_fusion.2
  516.5 8.7 %convolution_multiply_fusion = f32[4,64,2,512]{3,1,2,0:T(8,128)S(1)} fusion(bf16[2048,4,64,1]{0,2,3,1:T(8,128)(2,1)S(1)} %bitcast.161, bf16[4,2,512,2048]{2,3,1,0:T(8,128)(2,1)} %fusion.2), kind=kOutput, calls=%fused_computation.85 | convolution fusion | flops 1074003968 | bytes 18874368 | tf_op jit(solution)/shard_map/gjqk,kgd->qgjd/dot_general | solution.py:332
  526.2 27.8 %reduce-scatter.13.cloned.1.call-done = bf16[512,512]{0,1:T(8,128)(2,1)} async-done(((bf16[2048,512]{0,1:T(8,128)(2,1)}), bf16[512,512]{0,1:T(8,128)(2,1)}) %reduce-scatter.13.cloned.1.call-update) | async-done | bytes 524304 | tf_op jit(solution)/shard_map/reduce_scatter | solution.py:346
  556.0 3.0 fusion.90
  560.5 22.1 %reduce-scatter.19.cloned.1.call-done = bf16[1,4,64,640]{3,2,1,0:T(8,128)(2,1)} async-done(((bf16[4,4,64,640]{3,2,1,0:T(8,128)(2,1)}), bf16[1,4,64,640]{3,2,1,0:T(8,128)(2,1)}) %reduce-scatter.19.cloned.1.call-update) | async-done | bytes 327696 | tf_op jit(solution)/shard_map/reduce_scatter | solution.py:87
  582.9 2.6 convolution_convert_fusion.1
  585.6 2.5 fusion.43
  589.7 4.4 copy.188
  594.7 35.1 %reduce-scatter.11.cloned.1.call-done = bf16[512,1024]{1,0:T(8,128)(2,1)} async-done(((bf16[2048,1024]{1,0:T(8,128)(2,1)}), bf16[512,1024]{1,0:T(8,128)(2,1)}) %reduce-scatter.11.cloned.1.call-update) | async-done | bytes 1048592 | tf_op jit(solution)/shard_map/reduce_scatter | solution.py:294
  631.2 20.7 %reduce-scatter.21.cloned.1.call-done = bf16[1,64,640]{2,1,0:T(8,128)(2,1)} async-done(((bf16[4,64,640]{2,1,0:T(8,128)(2,1)}), bf16[1,64,640]{2,1,0:T(8,128)(2,1)}) %reduce-scatter.21.cloned.1.call-update) | async-done | bytes 81936 | tf_op jit(solution)/shard_map/reduce_scatter | solution.py:93
  654.8 31.0 %reduce-scatter.15.cloned.1.call-done = bf16[1,4,64,1152]{3,2,1,0:T(8,128)(2,1)} async-done(((bf16[4,4,64,1152]{3,2,1,0:T(8,128)(2,1)}), bf16[1,4,64,1152]{3,2,1,0:T(8,128)(2,1)}) %reduce-scatter.15.cloned.1.call-update) | async-done | bytes 589840 | tf_op jit(solution)/shard_map/reduce_scatter | solution.py:87
  685.8 4.1 fusion.52
  690.0 2.7 fusion.51
  692.7 106.2 %reduce-scatter.23.cloned.1.call-done = bf16[256,3072]{1,0:T(8,128)(2,1)} async-done(((bf16[1024,3072]{1,0:T(8,128)(2,1)}), bf16[256,3072]{1,0:T(8,128)(2,1)}) %reduce-scatter.23.cloned.1.call-update) | async-done | bytes 1572880 | tf_op jit(solution)/shard_map/reduce_scatter | solution.py:295
  801.7 22.1 %reduce-scatter.17.cloned.1.call-done = bf16[1,64,1152]{2,1,0:T(8,128)(2,1)} async-done(((bf16[4,64,1152]{2,1,0:T(8,128)(2,1)}), bf16[1,64,1152]{2,1,0:T(8,128)(2,1)}) %reduce-scatter.17.cloned.1.call-update) | async-done | bytes 147472 | tf_op jit(solution)/shard_map/reduce_scatter | solution.py:93
  831.0 5.6 collective-permute-done.9
  837.5 2.4 collective-permute-done.10
  840.6 3.2 reshape.271
  (209 shorter events, 67.3 us)
Async XLA Ops:
  7.2 28.3 %copy-start.2 = (bf16[1,512,1024]{2,1,0:T(8,128)(2,1)S(1)}, bf16[1,512,1024]{2,1,0:T(8,128)(2,1)}, u32[]{:S(2)}) copy-start(bf16[1,512,1024]{2,1,0:T(8,128)(2,1)} %param.13) | copy-start | bytes 3145732
  7.2 28.3 %all-gather.6.cloned.1.call-start = ((), (), s32[]{:S(2)}) async-start(), calls=%async_computation.8 | async-start | bytes 2621440 | tf_op jit(solution)/shard_map/all_gather | solution.py:127
  9.3 77.9 %all-gather.8.cloned.1.call-start = ((), (), s32[]{:S(2)}) async-start(), calls=%async_computation.9 | async-start | bytes 2621440 | tf_op jit(solution)/shard_map/all_gather | solution.py:175
  10.0 28.4 %copy-start.36 = (f32[1024]{0:T(1024)}, f32[1024]{0:T(1024)S(1)}, u32[]{:S(2)}) copy-start(f32[1024]{0:T(1024)S(1)} %convert_element_type.216) | copy-start | bytes 12292
  12.1 26.3 %copy-start.38 = (f32[512]{0:T(512)}, f32[512]{0:T(512)S(1)}, u32[]{:S(2)}) copy-start(f32[512]{0:T(512)S(1)} %add_rsqrt_fusion.1) | copy-start | bytes 6148
  12.4 36.3 %copy-start.20 = (f32[512,32]{0,1:T(8,128)}, f32[512,32]{0,1:T(8,128)S(1)}, u32[]{:S(2)}) copy-start(f32[512,32]{0,1:T(8,128)S(1)} %get-tuple-element.131) | copy-start | bytes 196612
  12.5 36.3 %copy-start.22 = (f32[512,32]{0,1:T(8,128)}, f32[512,32]{0,1:T(8,128)S(1)}, u32[]{:S(2)}) copy-start(f32[512,32]{0,1:T(8,128)S(1)} %get-tuple-element.132) | copy-start | bytes 196612
  38.4 1.3 copy-start.24
  40.0 2.7 copy-start.40
  40.0 3.5 copy-start.13
  41.1 94.2 %all-gather.10.cloned.1.call-start = ((), (), s32[]{:S(2)}) async-start(), calls=%async_computation.10 | async-start | bytes 1638400 | tf_op jit(solution)/shard_map/all_gather | solution.py:132
  41.2 4.1 copy-start.41
  42.7 227.6 %all-gather.12.cloned.1.call-start = ((), (), s32[]{:S(2)}) async-start(), calls=%async_computation.11 | async-start | bytes 5898240 | tf_op jit(solution)/shard_map/all_gather | solution.py:151
  44.7 225.6 %all-gather.14.cloned.1.call-start = ((), (), s32[]{:S(2)}) async-start(), calls=%async_computation.12 | async-start | bytes 5242880 | tf_op jit(solution)/shard_map/all_gather | solution.py:212
  49.6 42.8 %copy-start.26 = (bf16[512,8,32]{0,2,1:T(8,128)(2,1)}, bf16[512,8,32]{0,2,1:T(8,128)(2,1)S(1)}, u32[]{:S(2)}) copy-start(bf16[512,8,32]{0,2,1:T(8,128)(2,1)S(1)} %get-tuple-element.121) | copy-start | bytes 786436
  90.5 17.1 %copy-start.11 = (bf16[2048,256]{0,1:T(8,128)(2,1)}, bf16[2048,256]{0,1:T(8,128)(2,1)S(1)}, u32[]{:S(2)}) copy-start(bf16[2048,256]{0,1:T(8,128)(2,1)S(1)} %copy.166) | copy-start | bytes 3145732
  92.4 29.2 %copy-start.8 = (bf16[2048,256]{0,1:T(8,128)(2,1)}, bf16[2048,256]{0,1:T(8,128)(2,1)S(1)}, u32[]{:S(2)}) copy-start(bf16[2048,256]{0,1:T(8,128)(2,1)S(1)} %copy.165) | copy-start | bytes 3145732
  135.3 3.5 copy-start.30
  135.3 3.5 copy-start.42
  137.5 24.7 %collective-permute-start = (bf16[512,1024]{1,0:T(8,128)(2,1)S(1)}, bf16[512,1024]{1,0:T(8,128)(2,1)S(1)}, u32[]{:S(2)}, u32[]{:S(2)}) collective-permute-start(bf16[512,1024]{1,0:T(8,128)(2,1)S(1)} %convolution_convert_fusion.3), channel_id=1, source_target_pairs={{0,1},{1,0},{2,3},{3,2},{4,5},{5,4},{6,7},{7,6},{8,9},{9,8},{10,11... | collective-permute-start | bytes 3145736 | tf_op jit(solution)/shard_map/ppermute | solution.py:62
  164.0 228.8 %reduce-scatter.9.cloned.1.call-start = ((), (), s32[]{:S(2)}) async-start(), calls=%async_computation.13 | async-start | bytes 5898240 | tf_op jit(solution)/shard_map/reduce_scatter | solution.py:257
  178.7 51.2 %collective-permute-start.1 = (bf16[1,256,3072]{1,2,0:T(8,128)(2,1)}, bf16[1,256,3072]{1,2,0:T(8,128)(2,1)}, u32[]{:S(2)}, u32[]{:S(2)}) collective-permute-start(bf16[1,256,3072]{1,2,0:T(8,128)(2,1)} %get-tuple-element.108), channel_id=1, source_target_pairs={{0,8},{8,16},{16,24},{24,0},{1,9},{9,17},{17,25},{25,1},{2,10},{10... | collective-permute-start | bytes 4718600 | tf_op jit(solution)/shard_map/ppermute | solution.py:81
  178.7 53.8 %collective-permute-start.2 = (bf16[1,256,3072]{1,2,0:T(8,128)(2,1)}, bf16[1,256,3072]{1,2,0:T(8,128)(2,1)}, u32[]{:S(2)}, u32[]{:S(2)}) collective-permute-start(bf16[1,256,3072]{1,2,0:T(8,128)(2,1)} %get-tuple-element.107), channel_id=1, source_target_pairs={{0,16},{8,24},{16,0},{24,8},{1,17},{9,25},{17,1},{25,9},{2,18},{10... | collective-permute-start | bytes 4718600 | tf_op jit(solution)/shard_map/ppermute | solution.py:81
  180.4 81.4 %collective-permute-start.3 = (bf16[1,256,3072]{1,2,0:T(8,128)(2,1)}, bf16[1,256,3072]{1,2,0:T(8,128)(2,1)}, u32[]{:S(2)}, u32[]{:S(2)}) collective-permute-start(bf16[1,256,3072]{1,2,0:T(8,128)(2,1)} %get-tuple-element.106), channel_id=1, source_target_pairs={{0,24},{8,0},{16,8},{24,16},{1,25},{9,1},{17,9},{25,17},{2,26},{10... | collective-permute-start | bytes 4718600 | tf_op jit(solution)/shard_map/ppermute | solution.py:81
  184.5 3.5 copy-start.5
  264.3 2.8 copy-start.6
  267.1 2.0 copy-start.7
  339.0 215.1 %reduce-scatter.13.cloned.1.call-start = ((), (), s32[]{:S(2)}) async-start(), calls=%async_computation.15 | async-start | bytes 2621440 | tf_op jit(solution)/shard_map/reduce_scatter | solution.py:346
  340.0 9.5 %copy-start.9 = (bf16[2048,1024]{0,1:T(8,128)(2,1)S(1)}, bf16[2048,1024]{0,1:T(8,128)(2,1)}, u32[]{:S(2)}) copy-start(bf16[2048,1024]{0,1:T(8,128)(2,1)} %get-tuple-element.102) | copy-start | bytes 12582916
  340.0 9.5 %copy-start.10 = (bf16[2048,1024]{0,1:T(8,128)(2,1)S(1)}, bf16[2048,1024]{0,1:T(8,128)(2,1)}, u32[]{:S(2)}) copy-start(bf16[2048,1024]{0,1:T(8,128)(2,1)} %get-tuple-element.103) | copy-start | bytes 12582916
  366.6 27.7 %copy-start.4 = (bf16[512,1024]{1,0:T(8,128)(2,1)S(1)}, bf16[512,1024]{1,0:T(8,128)(2,1)}, u32[]{:S(2)}) copy-start(bf16[512,1024]{1,0:T(8,128)(2,1)} %multiply_convert_fusion.3) | copy-start | bytes 3145732
  392.8 28.0 %collective-permute-start.4 = (bf16[512,1152]{1,0:T(8,128)(2,1)}, bf16[512,1152]{1,0:T(8,128)(2,1)}, u32[]{:S(2)}, u32[]{:S(2)}) collective-permute-start(bf16[512,1152]{1,0:T(8,128)(2,1)} %reduce-scatter.9.cloned.1.call-done), channel_id=1, source_target_pairs={{0,1},{1,0},{2,3},{3,2},{4,5},{5,4},{6,7},{7,6},{8,9},{9,8},{10,11... | collective-permute-start | bytes 3538952 | tf_op jit(solution)/shard_map/ppermute | solution.py:62
  405.9 16.8 %copy-start.17 = (f32[512,16]{1,0:T(8,128)S(1)}, f32[512,16]{1,0:T(8,128)}, u32[]{:S(2)}) copy-start(f32[512,16]{1,0:T(8,128)} %copy-done.16) | copy-start | bytes 98308
  405.9 17.1 %copy-start.29 = (bf16[1024,640]{0,1:T(8,128)(2,1)S(1)}, bf16[1024,640]{0,1:T(8,128)(2,1)}, u32[]{:S(2)}) copy-start(bf16[1024,640]{0,1:T(8,128)(2,1)} %all-gather.10.cloned.1.call-done) | copy-start | bytes 3932164
  422.7 1.5 copy-start.15
  423.0 1.7 copy-start.14
  425.5 1.3 copy-start
  467.1 27.7 %copy-start.27 = (bf16[512,8,32]{0,2,1:T(8,128)(2,1)S(1)}, bf16[512,8,32]{0,2,1:T(8,128)(2,1)}, u32[]{:S(2)}) copy-start(bf16[512,8,32]{0,2,1:T(8,128)(2,1)} %copy-done.26) | copy-start | bytes 786436
  506.8 3.3 copy-start.18
  510.1 72.5 %reduce-scatter.19.cloned.1.call-start = ((), (), s32[]{:S(2)}) async-start(), calls=%async_computation.18 | async-start | bytes 1638400 | tf_op jit(solution)/shard_map/reduce_scatter | solution.py:87
  510.1 1.7 copy-start.1
  515.1 1.4 copy-start.12
  515.2 114.6 %reduce-scatter.11.cloned.1.call-start = ((), (), s32[]{:S(2)}) async-start(), calls=%async_computation.14 | async-start | bytes 5242880 | tf_op jit(solution)/shard_map/reduce_scatter | solution.py:294
  515.9 9.3 %copy-start.21 = (f32[512,32]{0,1:T(8,128)S(1)}, f32[512,32]{0,1:T(8,128)}, u32[]{:S(2)}) copy-start(f32[512,32]{0,1:T(8,128)} %copy-done.20) | copy-start | bytes 196612
  515.9 9.3 %copy-start.23 = (f32[512,32]{0,1:T(8,128)S(1)}, f32[512,32]{0,1:T(8,128)}, u32[]{:S(2)}) copy-start(f32[512,32]{0,1:T(8,128)} %copy-done.22) | copy-start | bytes 196612
  515.9 136.0 %reduce-scatter.21.cloned.1.call-start = ((), (), s32[]{:S(2)}) async-start(), calls=%async_computation.19 | async-start | bytes 409600 | tf_op jit(solution)/shard_map/reduce_scatter | solution.py:93
  554.1 1.4 copy-start.31
  554.1 1.9 copy-start.43
  555.3 3.7 copy-start.35
  556.0 26.9 %copy-start.3 = (bf16[1,512,1024]{2,1,0:T(8,128)(2,1)S(1)}, bf16[1,512,1024]{2,1,0:T(8,128)(2,1)}, u32[]{:S(2)}) copy-start(bf16[1,512,1024]{2,1,0:T(8,128)(2,1)} %param.13) | copy-start | bytes 3145732
  556.0 26.9 %copy-start.37 = (f32[1024]{0:T(1024)S(1)}, f32[1024]{0:T(1024)}, u32[]{:S(2)}) copy-start(f32[1024]{0:T(1024)} %copy-done.36) | copy-start | bytes 12292
  556.0 26.9 %copy-start.39 = (f32[512]{0:T(512)S(1)}, f32[512]{0:T(512)}, u32[]{:S(2)}) copy-start(f32[512]{0:T(512)} %copy-done.38) | copy-start | bytes 6148
  559.0 26.6 %collective-permute-start.6 = (bf16[512,1024]{1,0:T(8,128)(2,1)}, bf16[512,1024]{1,0:T(8,128)(2,1)}, u32[]{:S(2)}, u32[]{:S(2)}) collective-permute-start(bf16[512,1024]{1,0:T(8,128)(2,1)} %get-tuple-element.143), channel_id=1, source_target_pairs={{0,1},{1,0},{2,3},{3,2},{4,5},{5,4},{6,7},{7,6},{8,9},{9,8},{10,11... | collective-permute-start | bytes 3145736 | tf_op jit(solution)/shard_map/ppermute | solution.py:62
  582.6 103.2 %reduce-scatter.15.cloned.1.call-start = ((), (), s32[]{:S(2)}) async-start(), calls=%async_computation.16 | async-start | bytes 2949120 | tf_op jit(solution)/shard_map/reduce_scatter | solution.py:87
  582.9 2.7 copy-start.19
  594.0 204.8 %reduce-scatter.23.cloned.1.call-start = ((), (), s32[]{:S(2)}) async-start(), calls=%async_computation.20 | async-start | bytes 7864320 | tf_op jit(solution)/shard_map/reduce_scatter | solution.py:295
  594.6 229.2 %reduce-scatter.17.cloned.1.call-start = ((), (), s32[]{:S(2)}) async-start(), calls=%async_computation.17 | async-start | bytes 737280 | tf_op jit(solution)/shard_map/reduce_scatter | solution.py:93
  629.7 60.2 %collective-permute-start.5 = (bf16[512,1024]{1,0:T(8,128)(2,1)}, bf16[512,1024]{1,0:T(8,128)(2,1)}, u32[]{:S(2)}, u32[]{:S(2)}) collective-permute-start(bf16[512,1024]{1,0:T(8,128)(2,1)} %reduce-scatter.11.cloned.1.call-done), channel_id=1, source_target_pairs={{0,1},{1,0},{2,3},{3,2},{4,5},{5,4},{6,7},{7,6},{8,9},{9,8},{10,11... | collective-permute-start | bytes 3145736 | tf_op jit(solution)/shard_map/ppermute | solution.py:62
  685.8 4.1 copy-start.28
  798.9 2.0 copy-start.25
  801.7 28.6 %collective-permute-start.8 = (bf16[1,64,3072]{2,1,0:T(8,128)(2,1)S(1)}, bf16[1,64,3072]{2,1,0:T(8,128)(2,1)S(1)}, u32[]{:S(2)}, u32[]{:S(2)}) collective-permute-start(bf16[1,64,3072]{2,1,0:T(8,128)(2,1)S(1)} %get-tuple-element.117), channel_id=1, source_target_pairs={{0,8},{8,16},{16,24},{24,0},{1,9},{9,17},{17,25},{25,1},{2,10},{10... | collective-permute-start | bytes 1179656 | tf_op jit(solution)/shard_map/ppermute | solution.py:81
  825.4 4.2 collective-permute-start.7
  828.1 8.5 collective-permute-start.9
  830.2 9.6 %collective-permute-start.10 = (bf16[1,64,3072]{2,1,0:T(8,128)(2,1)S(1)}, bf16[1,64,3072]{2,1,0:T(8,128)(2,1)S(1)}, u32[]{:S(2)}, u32[]{:S(2)}) collective-permute-start(bf16[1,64,3072]{2,1,0:T(8,128)(2,1)S(1)} %get-tuple-element.115), channel_id=1, source_target_pairs={{0,24},{8,0},{16,8},{24,16},{1,25},{9,1},{17,9},{25,17},{2,26},{10... | collective-permute-start | bytes 1179656 | tf_op jit(solution)/shard_map/ppermute | solution.py:81
  (4 other events, 3.3 us)
Sparse Core Ops, SparseCore 0:
  10.2 25.2 all-gather.5
  41.2 45.9 all-gather.7
  88.8 17.0 all-gather.9
  107.3 37.4 all-gather.11
  164.1 48.2 all-gather.13
  339.1 53.6 reduce-scatter.8
  510.2 43.8 reduce-scatter.12
  556.6 25.8 reduce-scatter.18
  585.2 44.4 reduce-scatter.10
  631.9 19.9 reduce-scatter.20
  654.4 31.3 reduce-scatter.14
  688.1 110.7 reduce-scatter.22
  801.2 22.4 reduce-scatter.16
